TPU v7x, 32 devices: a whole 2x2x4 slice. The times are simulated.
32 devices in a mesh: replica: 4 (over y, x), group: 8 (over z, core).
Axes of the slice: x: 2, y: 2, z: 4, core: 2. Of those that a mesh axis runs over, the one named last changes fastest.
Arguments:
- tokens: bfloat16 [64, 512, 768], P(('replica', 'group')), may hold values from -6 to 6
- lengths: int32 [64], replicated, may hold values from 1 to 512, as said below
- slot_order: int32 [64], P(('replica', 'group')), may hold values from 0 to 63, each once
- qkv_weight: bfloat16 [768, 2304], P('replica'), may hold values from -0.21875 to 0.21875
- qv_bias: bfloat16 [1536], P('replica'), may hold values from -3 to 3
- out_weight: bfloat16 [768, 768], P('replica'), may hold values from -2.5 to 2.5
- out_bias: bfloat16 [768], P('replica'), may hold values from -3 to 3
- attn_gain: bfloat16 [768], P('replica'), may hold values from 0.25 to 1.75
- attn_shift: bfloat16 [768], P('replica'), may hold values from -3 to 3
- up_weight: bfloat16 [768, 3072], P('replica'), may hold values from -0.21875 to 0.21875
- up_bias: bfloat16 [3072], P('replica'), may hold values from -3 to 3
- down_weight: bfloat16 [3072, 768], P('replica'), may hold values from -0.109375 to 0.109375
- down_bias: bfloat16 [768], P('replica'), may hold values from -3 to 3
- mlp_gain: bfloat16 [768], P('replica'), may hold values from 0.25 to 1.75
- mlp_shift: bfloat16 [768], P('replica'), may hold values from -3 to 3
- cotangent: bfloat16 [64, 512, 768], P(('replica', 'group')), may hold values from -6 to 6
Outputs:
- layer_out: bfloat16 [64, 512, 768], P(('replica', 'group'))
- grad_tokens: bfloat16 [64, 512, 768], P(('replica', 'group'))
- grad_qkv_weight: float32 [768, 2304], P('replica')
- grad_qv_bias: float32 [1536], P('replica')
- grad_out_weight: float32 [768, 768], P('replica')
- grad_out_bias: float32 [768], P('replica')
- grad_attn_gain: float32 [768], P('replica')
- grad_attn_shift: float32 [768], P('replica')
- grad_up_weight: float32 [768, 3072], P('replica')
- grad_up_bias: float32 [3072], P('replica')
- grad_down_weight: float32 [3072, 768], P('replica')
- grad_down_bias: float32 [768], P('replica')
- grad_mlp_gain: float32 [768], P('replica')
- grad_mlp_shift: float32 [768], P('replica')
Inputs may be any that keep to these rules, and one draw needn't show every extreme that they name: `lengths`: some sequence has exactly 512 tokens and some has exactly 1. `slot_order`: A permutation of the 64 sequences over the slots.
All inputs are finite; a program needn't handle non-finite values.
Results may differ from a plain program's by a relative error of at most 0.02.
Values may be sent and summed in bfloat16 or wider, within the bound.
A program may use at most 192 MiB of HBM per device.

v0:
```python
import jax
import jax.numpy as jnp
from jax import lax
from jax.sharding import PartitionSpec as P

HEADS = 12


def as_sent(shard):

    def short(part):
        return part.astype(jnp.bfloat16) if part.dtype == jnp.float32 else part

    return jax.tree.map(short, shard)


def layer_norm(row_data, gain_row, shift_row):
    row_mean = jnp.mean(row_data, axis=-1, keepdims=True)
    centred = row_data - row_mean
    spread = jnp.mean(centred * centred, axis=-1, keepdims=True)
    return centred * lax.rsqrt(spread + 1e-06) * gain_row + shift_row


def gelu_exact(values):
    return 0.5 * values * (1.0 + lax.erf(values * 0.7071067811865476))


def weight_grad(left, right):
    return lax.dot_general(
        left, right, (((0,), (0,)), ((), ())), preferred_element_type=jnp.float32
    )


def back_product(grad_rows, weight):
    return lax.dot_general(
        grad_rows, weight, (((1,), (1,)), ((), ())), preferred_element_type=jnp.float32
    )


def column_sum(grad_rows):
    return jnp.sum(grad_rows.astype(jnp.float32), axis=0)


def body(
    tokens,
    lengths,
    slot_order,
    qkv_weight,
    qv_bias,
    out_weight,
    out_bias,
    attn_gain,
    attn_shift,
    up_weight,
    up_bias,
    down_weight,
    down_bias,
    mlp_gain,
    mlp_shift,
    cotangent,
):
    slot_count, seqlen, model_width = tokens.shape
    head_count = HEADS
    head_size = model_width // head_count
    score_scale = head_size ** (-0.5)
    row_count = slot_count * seqlen
    picked = slot_order[:, None] == jnp.arange(lengths.shape[0], dtype=jnp.int32)[None, :]
    slot_lens = jnp.sum(jnp.where(picked, lengths[None, :], 0), axis=1)
    valid_keys = jnp.arange(seqlen, dtype=jnp.int32)[None, :] < slot_lens[:, None]
    row_valid = valid_keys.reshape(row_count, 1).astype(jnp.float32)
    attn_full = (
        lax.all_gather(qkv_weight, "replica", axis=0, tiled=True),
        lax.all_gather(qv_bias, "replica", axis=0, tiled=True),
        lax.all_gather(out_weight, "replica", axis=0, tiled=True),
        lax.all_gather(out_bias, "replica", axis=0, tiled=True),
        lax.all_gather(attn_gain, "replica", axis=0, tiled=True),
        lax.all_gather(attn_shift, "replica", axis=0, tiled=True),
    )
    flat_rows = tokens.reshape(row_count, model_width)
    full_qkv, full_qv, full_out, full_outb, full_gain, full_shift = attn_full
    qv_float = full_qv.astype(jnp.float32)
    bias_row = jnp.concatenate(
        [qv_float[:model_width], jnp.zeros((model_width,), jnp.float32), qv_float[model_width:]]
    )
    projected = (
        jnp.dot(flat_rows, full_qkv, preferred_element_type=jnp.float32) + bias_row
    ).astype(jnp.bfloat16)
    stacked = projected.reshape(slot_count, seqlen, 3, head_count, head_size)

    def attend_slot(items):
        triple, slot_valid = items
        queries = triple[:, 0]
        key_rows = triple[:, 1]
        values = triple[:, 2]
        scores = (
            jnp.einsum("qhd,khd->hqk", queries, key_rows, preferred_element_type=jnp.float32)
            * score_scale
        )
        scores = jnp.where(slot_valid[None, None, :], scores, -1e30)
        row_max = jnp.max(scores, axis=-1, keepdims=True)
        exp_scores = jnp.exp(scores - row_max)
        row_total = jnp.sum(exp_scores, axis=-1, keepdims=True)
        soft_weights = (exp_scores / row_total).astype(jnp.bfloat16)
        context = jnp.einsum(
            "hqk,khd->qhd", soft_weights, values, preferred_element_type=jnp.float32
        )
        return (
            context.reshape(seqlen, model_width).astype(jnp.bfloat16),
            (row_max + jnp.log(row_total))[:, :, 0],
        )

    contexts, log_totals = lax.map(attend_slot, (stacked, valid_keys))
    context_rows = contexts.reshape(row_count, model_width)
    attn_out = jnp.dot(
        context_rows, full_out, preferred_element_type=jnp.float32
    ) + full_outb.astype(jnp.float32)
    residual_first = flat_rows.astype(jnp.float32) + attn_out
    stacked, log_totals, context_rows, residual_first = (
        stacked,
        log_totals,
        context_rows,
        residual_first,
    )
    first_gain = attn_full[4].astype(jnp.float32)
    first_shift = attn_full[5].astype(jnp.float32)
    hidden = layer_norm(residual_first, first_gain, first_shift)
    hidden_low = hidden.astype(jnp.bfloat16)
    mlp_full = (
        lax.all_gather(up_weight, "replica", axis=0, tiled=True),
        lax.all_gather(up_bias, "replica", axis=0, tiled=True),
        lax.all_gather(down_weight, "replica", axis=0, tiled=True),
        lax.all_gather(down_bias, "replica", axis=0, tiled=True),
        lax.all_gather(mlp_gain, "replica", axis=0, tiled=True),
        lax.all_gather(mlp_shift, "replica", axis=0, tiled=True),
    )
    pre_act = jnp.dot(hidden_low, mlp_full[0], preferred_element_type=jnp.float32) + mlp_full[
        1
    ].astype(jnp.float32)
    activ_low = gelu_exact(pre_act).astype(jnp.bfloat16)
    down_out = jnp.dot(activ_low, mlp_full[2], preferred_element_type=jnp.float32) + mlp_full[
        3
    ].astype(jnp.float32)
    residual_second = hidden + down_out
    second_gain = mlp_full[4].astype(jnp.float32)
    second_shift = mlp_full[5].astype(jnp.float32)
    normed = layer_norm(residual_second, second_gain, second_shift)
    layer_out = (normed * row_valid).astype(jnp.bfloat16).reshape(slot_count, seqlen, model_width)
    mlp_back = (
        lax.all_gather(up_weight, "replica", axis=0, tiled=True),
        lax.all_gather(up_bias, "replica", axis=0, tiled=True),
        lax.all_gather(down_weight, "replica", axis=0, tiled=True),
        lax.all_gather(down_bias, "replica", axis=0, tiled=True),
        lax.all_gather(mlp_gain, "replica", axis=0, tiled=True),
        lax.all_gather(mlp_shift, "replica", axis=0, tiled=True),
    )
    grad_out = cotangent.reshape(row_count, model_width).astype(jnp.float32) * row_valid
    unused_second, second_pull = jax.vjp(layer_norm, residual_second, second_gain, second_shift)
    grad_res_second, grad_mlp_gain, grad_mlp_shift = second_pull(grad_out)
    grad_down_low = grad_res_second.astype(jnp.bfloat16)
    grad_down_weight = weight_grad(activ_low, grad_down_low)
    grad_down_bias = column_sum(grad_down_low)
    grad_activ = back_product(grad_down_low, mlp_back[2])
    unused_act, gelu_pull = jax.vjp(gelu_exact, pre_act)
    grad_pre_low = gelu_pull(grad_activ)[0].astype(jnp.bfloat16)
    grad_up_weight = weight_grad(hidden_low, grad_pre_low)
    grad_up_bias = column_sum(grad_pre_low)
    grad_hidden = grad_res_second + back_product(grad_pre_low, mlp_back[0])
    mlp_terms = (
        grad_up_weight,
        grad_up_bias,
        grad_down_weight,
        grad_down_bias,
        grad_mlp_gain,
        grad_mlp_shift,
    )
    attn_back = (
        lax.all_gather(qkv_weight, "replica", axis=0, tiled=True),
        lax.all_gather(qv_bias, "replica", axis=0, tiled=True),
        lax.all_gather(out_weight, "replica", axis=0, tiled=True),
        lax.all_gather(out_bias, "replica", axis=0, tiled=True),
        lax.all_gather(attn_gain, "replica", axis=0, tiled=True),
        lax.all_gather(attn_shift, "replica", axis=0, tiled=True),
    )
    unused_first, first_pull = jax.vjp(layer_norm, residual_first, first_gain, first_shift)
    grad_res_first, grad_attn_gain, grad_attn_shift = first_pull(grad_hidden)
    grad_attn_low = grad_res_first.astype(jnp.bfloat16)
    grad_out_weight = weight_grad(context_rows, grad_attn_low)
    grad_out_bias = column_sum(grad_attn_low)
    grad_context = back_product(grad_attn_low, attn_back[2]).astype(jnp.bfloat16)
    grad_context = grad_context.reshape(slot_count, seqlen, head_count, head_size)

    def attend_back(items):
        triple, slot_valid, log_total, grad_ctx = items
        queries = triple[:, 0]
        key_rows = triple[:, 1]
        values = triple[:, 2]
        scores = (
            jnp.einsum("qhd,khd->hqk", queries, key_rows, preferred_element_type=jnp.float32)
            * score_scale
        )
        soft_weights = jnp.where(
            slot_valid[None, None, :], jnp.exp(scores - log_total[:, :, None]), 0.0
        )
        grad_values = jnp.einsum(
            "hqk,qhd->khd",
            soft_weights.astype(jnp.bfloat16),
            grad_ctx,
            preferred_element_type=jnp.float32,
        )
        grad_soft = jnp.einsum("qhd,khd->hqk", grad_ctx, values, preferred_element_type=jnp.float32)
        inner = jnp.sum(soft_weights * grad_soft, axis=-1, keepdims=True)
        grad_scores = (soft_weights * (grad_soft - inner)).astype(jnp.bfloat16)
        grad_queries = (
            jnp.einsum("hqk,khd->qhd", grad_scores, key_rows, preferred_element_type=jnp.float32)
            * score_scale
        )
        grad_keys = (
            jnp.einsum("hqk,qhd->khd", grad_scores, queries, preferred_element_type=jnp.float32)
            * score_scale
        )
        return jnp.stack([grad_queries, grad_keys, grad_values], axis=1).astype(jnp.bfloat16)

    grad_proj = lax.map(attend_back, (stacked, valid_keys, log_totals, grad_context)).reshape(
        row_count, 3 * model_width
    )
    grad_qkv_weight = weight_grad(flat_rows, grad_proj)
    proj_sums = column_sum(grad_proj)
    grad_qv_bias = jnp.concatenate([proj_sums[:model_width], proj_sums[2 * model_width :]])
    grad_tokens = (grad_res_first + back_product(grad_proj, attn_back[0])).astype(jnp.bfloat16)
    grad_tokens = grad_tokens.reshape(slot_count, seqlen, model_width)
    attn_terms = (
        grad_qkv_weight,
        grad_qv_bias,
        grad_out_weight,
        grad_out_bias,
        grad_attn_gain,
        grad_attn_shift,
    )
    shares = jax.tree.map(
        lambda part: part.astype(jnp.float32),
        lax.psum_scatter(
            as_sent(attn_terms + mlp_terms), "replica", scatter_dimension=0, tiled=True
        ),
    )
    totals = tuple(
        jax.tree.map(lambda part: part.astype(jnp.float32), lax.psum(as_sent(shares), "group"))
    )
    return (
        layer_out,
        grad_tokens,
        totals[0],
        totals[1],
        totals[2],
        totals[3],
        totals[4],
        totals[5],
        totals[6],
        totals[7],
        totals[8],
        totals[9],
        totals[10],
        totals[11],
    )


def solution(mesh):
    return jax.shard_map(
        body,
        mesh=mesh,
        in_specs=(
            P(("replica", "group"), None, None),
            P(),
            P(("replica", "group")),
            P("replica", None),
            P("replica"),
            P("replica", None),
            P("replica"),
            P("replica"),
            P("replica"),
            P("replica", None),
            P("replica"),
            P("replica", None),
            P("replica"),
            P("replica"),
            P("replica"),
            P(("replica", "group"), None, None),
        ),
        out_specs=(
            P(("replica", "group"), None, None),
            P(("replica", "group"), None, None),
            P("replica", None),
            P("replica"),
            P("replica", None),
            P("replica"),
            P("replica"),
            P("replica"),
            P("replica", None),
            P("replica"),
            P("replica", None),
            P("replica"),
            P("replica"),
            P("replica"),
        ),
        check_vma=False,
    )
```

profile of v0, /device:TPU:0, one launch (start us, length us, event | category | flops | bytes accessed | tf_op | source)
XLA Modules:
  0.0 639.5 jit_solution(14011597038286033600)
XLA Ops:
  12.6 17.8 %all-reduce.17 = (bf16[768]{0:T(1024)(128)(2,1)S(1)}, bf16[768]{0:T(1024)(128)(2,1)S(1)}, bf16[768]{0:T(1024)(128)(2,1)S(1)}, bf16[768]{0:T(1024)(128)(2,1)S(1)}, bf16[768]{0:T(1024)(128)(2,1)S(1)}) all-reduce(bf16[768]{0:T(1024)(128)(2,1)S(1)} %dynamic-update-slice, ...), channel_id=1, replica_groups=mesh['replica'=4,'group'=8] {'replica'}, use_global_device_ids=true, to_apply=%add | all-reduce | flops 3840 | bytes 15360
  30.4 7.0 %all-gather = bf16[4,1,384]{2,1,0:T(2,128)(2,1)S(1)} all-gather(bf16[1,1,384]{2,1,0:T(2,128)(2,1)S(1)} %reshape.268), channel_id=1, replica_groups=mesh['replica'=4,'group'=8] {'replica'}, dimensions={0}, use_global_device_ids=true | all-gather | bytes 3840 | tf_op jit(solution)/shard_map/all_gather | solution.py:73
  39.6 8.3 %all-gather.1 = bf16[4,1,768]{2,1,0:T(2,128)(2,1)S(1)} all-gather(bf16[1,1,768]{2,1,0:T(2,128)(2,1)S(1)} %reshape.270), channel_id=1, replica_groups=mesh['replica'=4,'group'=8] {'replica'}, dimensions={0}, use_global_device_ids=true | all-gather | bytes 7680 | tf_op jit(solution)/shard_map/all_gather | solution.py:130
  50.3 9.9 %all-gather.7.cloned.1.call-done = bf16[768,2304]{1,0:T(8,128)(2,1)} async-done(((bf16[192,2304]{1,0:T(8,128)(2,1)}), bf16[768,2304]{1,0:T(8,128)(2,1)}) %all-gather.7.cloned.1.call-update) | async-done | bytes 3538960 | tf_op jit(solution)/shard_map/all_gather | solution.py:72
  60.2 7.5 %add_convert_fusion.1 = bf16[1024,2304]{1,0:T(8,128)(2,1)} fusion(bf16[1024,768]{1,0:T(8,128)(2,1)S(1)} %bitcast.168, bf16[768,2304]{1,0:T(8,128)(2,1)} %all-gather.7.cloned.1.call-done, f32[2304]{0:T(1024)S(1)} %pad_maximum_fusion), kind=kOutput, calls=%fused_computation.49 | convolution fusion | flops 3628597248 | bytes 9839616 | tf_op jit(solution)/shard_map/dot_general | solution.py:86
  67.7 6.7 %copy.66 = bf16[1024,2304]{0,1:T(8,128)(2,1)} copy(bf16[1024,2304]{1,0:T(8,128)(2,1)} %add_convert_fusion.1) | data formatting | bytes 9437184 | tf_op jit(solution)/shard_map/convert_element_type | solution.py:87
  74.4 8.8 %reshape.242 = bf16[2,512,3,12,64]{1,0,4,3,2:T(2,128)(2,1)} reshape(bf16[1024,2304]{0,1:T(8,128)(2,1)} %copy.66) | data formatting | bytes 9437184 | tf_op jit(solution)/shard_map/reshape | solution.py:88
  83.2 5.6 copy.67
  88.9 22.9 %while.22 = (s32[]{:T(128)}, bf16[2,512,768]{2,1,0:T(8,128)(2,1)S(1)}, f32[2,12,512]{2,1,0:T(8,128)S(1)}, bf16[2,512,3,12,64]{1,4,3,2,0:T(8,128)(2,1)}, pred[2,512]{1,0:T(4,128)(4,1)S(1)}, /*index=5*/s32[]{:T(128)}) while((s32[]{:T(128)}, bf16[2,512,768]{2,1,0:T(8,128)(2,1)S(1)}, f32[2,12,512]{2,1,0:T(8,128)S(1)}, ...), condition=%wide.region_4.5_spmd, body=%wide.region_1.4_spmd.sunk | while | flops 843442176 | bytes 48998996 | solution.py:112
  90.9 3.1 fusion.83
  94.0 2.6 fusion.84
  96.6 3.3 fusion.85
  102.5 3.1 fusion.83
  105.5 2.6 fusion.84
  108.2 3.3 fusion.85
  112.9 3.8 fusion.45
  117.3 31.4 %all-gather.11.cloned.1.call-done = bf16[768,3072]{1,0:T(8,128)(2,1)} async-done(((bf16[192,3072]{1,0:T(8,128)(2,1)}), bf16[768,3072]{1,0:T(8,128)(2,1)}) %all-gather.11.cloned.1.call-update) | async-done | bytes 4718608 | tf_op jit(solution)/shard_map/all_gather | solution.py:129
  148.7 12.6 %multiply_convert_fusion.3 = (bf16[1024,3072]{1,0:T(8,128)(2,1)}, f32[1024,3072]{1,0:T(8,128)}) fusion(f32[3072]{0:T(1024)S(1)} %bitcast.161, bf16[768,3072]{1,0:T(8,128)(2,1)} %all-gather.11.cloned.1.call-done, f32[1024,768]{1,0:T(8,128)S(1)} %get-tuple-element.252, f32[768]{0:T(1024)S(1)} %copy-done.37, f32[768]{0:T(1024)S(1)} %copy-done.28, ...), kind=kOutput, calls=%fused_computation.47 | convolution fusion | flops 4854644736 | bytes 26765312 | tf_op jit(solution)/shard_map/dot_general | solution.py:136
  161.3 46.2 %all-gather.13.cloned.1.call-done = bf16[3072,768]{1,0:T(8,128)(2,1)} async-done(((bf16[768,768]{1,0:T(8,128)(2,1)}), bf16[3072,768]{1,0:T(8,128)(2,1)}) %all-gather.13.cloned.1.call-update) | async-done | bytes 4718608 | tf_op jit(solution)/shard_map/all_gather | solution.py:131
  207.5 8.8 %fusion.46 = (f32[1024]{0:T(1024)S(1)}, f32[1024,768]{1,0:T(8,128)S(1)}) fusion(f32[768]{0:T(1024)S(1)} %copy-done.39, bf16[1024,3072]{1,0:T(8,128)(2,1)} %get-tuple-element.253, bf16[3072,768]{1,0:T(8,128)(2,1)} %all-gather.13.cloned.1.call-done, f32[768]{0:T(1024)S(1)} %copy-done.37, f32[768]{0:T(1024)S(1)} %copy-done.28, f32[1024]{0:T(1024)S(1)} %fusion.32, ...), kind=kOutput, calls=%fused_computation.103 | convolution fusion | flops 4837342208 | bytes 17323008 | tf_op jit(solution)/shard_map/dot_general | solution.py:140
  223.8 15.2 %fusion.47 = (bf16[3072]{0:T(1024)(128)(2,1)}, bf16[1024,3072]{1,0:T(8,128)(2,1)S(1)}) fusion(bf16[1024,768]{1,0:T(8,128)(2,1)S(1)} %get-tuple-element.233, bf16[3072,768]{1,0:T(8,128)(2,1)S(1)} %bitcast.166, f32[1024,3072]{1,0:T(8,128)} %get-tuple-element.254, f32[3072]{0:T(1024)S(1)} %bitcast.162), kind=kOutput, calls=%fused_computation.104 | convolution fusion | flops 4879021056 | bytes 25184256 | tf_op jit(solution)/shard_map/dot_general | solution.py:35
  239.0 6.5 %multiply_reduce_fusion.3 = (bf16[768]{0:T(1024)(128)(2,1)}, f32[1024]{0:T(1024)S(1)}, bf16[768]{0:T(1024)(128)(2,1)}, f32[1024,768]{1,0:T(8,128)S(1)}) fusion(f32[1024,768]{1,0:T(8,128)S(1)} %get-tuple-element.252, f32[1024]{0:T(1024)S(1)} %fusion.32, f32[1024]{0:T(1024)S(1)} %broadcast_multiply_fusion.1, f32[768]{0:T(1024)S(1)} %copy-done.28, ...), kind=kOutput, calls=%fused_computation.59 | convolution fusion | flops 4839699456 | bytes 20469760 | tf_op jit(solution)/shard_map/dot_general | solution.py:35
  253.2 2.4 reshape.245
  257.3 49.9 %while.23 = (s32[]{:T(128)}, bf16[2,512,3,12,64]{1,4,3,2,0:T(8,128)(2,1)}, bf16[2,512,3,12,64]{1,4,3,2,0:T(8,128)(2,1)}, pred[2,512]{1,0:T(4,128)(4,1)S(1)}, f32...) while((s32[]{:T(128)}, bf16[2,512,3,12,64]{1,4,3,2,0:T(8,128)(2,1)}, ...), condition=%wide.region_15.16_spmd, body=%wide.region_13.15_spmd.sunk | while | flops 2069489664 | bytes 111864928 | solution.py:223
  261.0 6.5 %multiply_reduce_fusion.9 = (f32[12,512]{1,0:T(8,128)S(1)}, f32[12,512,512]{1,2,0:T(8,128)}) fusion(f32[12,512,512]{1,2,0:T(8,128)S(1)} %fusion.90, f32[12,512]{1,0:T(8,128)S(1)} %dynamic-slice_bitcast_fusion.8, pred[512]{0:T(512)(128)(4,1)S(1)} %dynamic-slice_reduce_fusion.5, bf16[512,3,12,64]{0,3,2,1:T(8,128)(2,1)S(1)} %dynamic-slice_bitcast_fusion.7, ...), kind=kOutput, calls=%fused_computation.18.clone.1 | convolution fusion | flops 418375680 | bytes 26796548 | tf_op jit(solution)/shard_map/while/body/eval_jaxpr/qhd,khd->hqk/dot_general | solution.py:210
  267.6 7.1 %multiply_convert_fusion.6 = bf16[12,512,512]{1,2,0:T(8,128)(2,1)S(1)} fusion(f32[12,512,512]{1,2,0:T(8,128)} %get-tuple-element.334, f32[12,512,512]{1,2,0:T(8,128)S(1)} %fusion.90, f32[12,512]{1,0:T(8,128)S(1)} %get-tuple-element.335, f32[12,512]{1,0:T(8,128)S(1)} %dynamic-slice_bitcast_fusion.8, pred[512]{0:T(512)(128)(4,1)S(1)} %dynamic-slice_reduce_fusion.5), kind=kLoop, calls=%fused_computation.17.clone.1 | loop fusion | flops 18874368 | bytes 31506944 | tf_op jit(solution)/shard_map/while/body/eval_jaxpr/convert_element_type | solution.py:212
  277.8 2.7 fusion.91
  285.8 6.5 %multiply_reduce_fusion.9 = (f32[12,512]{1,0:T(8,128)S(1)}, f32[12,512,512]{1,2,0:T(8,128)}) fusion(f32[12,512,512]{1,2,0:T(8,128)S(1)} %fusion.90, f32[12,512]{1,0:T(8,128)S(1)} %dynamic-slice_bitcast_fusion.8, pred[512]{0:T(512)(128)(4,1)S(1)} %dynamic-slice_reduce_fusion.5, bf16[512,3,12,64]{0,3,2,1:T(8,128)(2,1)S(1)} %dynamic-slice_bitcast_fusion.7, ...), kind=kOutput, calls=%fused_computation.18.clone.1 | convolution fusion | flops 418375680 | bytes 26796548 | tf_op jit(solution)/shard_map/while/body/eval_jaxpr/qhd,khd->hqk/dot_general | solution.py:210
  292.4 7.1 %multiply_convert_fusion.6 = bf16[12,512,512]{1,2,0:T(8,128)(2,1)S(1)} fusion(f32[12,512,512]{1,2,0:T(8,128)} %get-tuple-element.334, f32[12,512,512]{1,2,0:T(8,128)S(1)} %fusion.90, f32[12,512]{1,0:T(8,128)S(1)} %get-tuple-element.335, f32[12,512]{1,0:T(8,128)S(1)} %dynamic-slice_bitcast_fusion.8, pred[512]{0:T(512)(128)(4,1)S(1)} %dynamic-slice_reduce_fusion.5), kind=kLoop, calls=%fused_computation.17.clone.1 | loop fusion | flops 18874368 | bytes 31506944 | tf_op jit(solution)/shard_map/while/body/eval_jaxpr/convert_element_type | solution.py:212
  302.6 2.7 fusion.91
  307.1 9.4 %copy.72 = bf16[2,512,3,12,64]{1,0,4,3,2:T(2,128)(2,1)} copy(bf16[2,512,3,12,64]{1,4,3,2,0:T(8,128)(2,1)} %get-tuple-element.76) | data formatting | bytes 9437184 | tf_op jit(solution)/shard_map/while | solution.py:223
  316.5 4.0 copy.87
  322.6 4.0 fusion.29
  326.6 4.1 copy.78
  330.9 4.5 convolution_convert_fusion.4
  335.5 10.8 %convolution_convert_fusion.1 = bf16[768,3072]{1,0:T(8,128)(2,1)} fusion(bf16[1024,3072]{1,0:T(8,128)(2,1)} %copy-done.58, f32[1024,768]{1,0:T(8,128)S(1)} %copy-done.7, f32[768]{0:T(1024)S(1)} %copy-done.38, f32[768]{0:T(1024)S(1)} %copy-done.29, f32[1024]{0:T(1024)S(1)} %copy-done.31, f32[1024]{0:T(1024)S(1)} %copy-done.24), kind=kOutput, calls=%fused_computation.51 | convolution fusion | flops 4838129664 | bytes 14170112 | tf_op jit(solution)/shard_map/dot_general | solution.py:29
  347.7 9.9 %convolution_convert_fusion = bf16[3072,768]{1,0:T(8,128)(2,1)} fusion(bf16[1024,3072]{1,0:T(8,128)(2,1)} %get-tuple-element.253, bf16[1024,768]{1,0:T(8,128)(2,1)S(1)} %copy-done.10), kind=kOutput, calls=%fused_computation.50 | convolution fusion | flops 4834197504 | bytes 12582912 | tf_op jit(solution)/shard_map/dot_general | solution.py:29
  360.4 3.0 reduce.5
  363.5 14.6 %reduce-scatter.13.cloned.1.call-done = bf16[192,2304]{1,0:T(8,128)(2,1)} async-done(((bf16[768,2304]{1,0:T(8,128)(2,1)}), bf16[192,2304]{1,0:T(8,128)(2,1)}) %reduce-scatter.13.cloned.1.call-update) | async-done | bytes 884752
  378.1 2.3 copy.79
  380.5 29.6 %reduce-scatter.7.cloned.1.call-done = bf16[192,768]{1,0:T(8,128)(2,1)} async-done(((bf16[768,768]{1,0:T(8,128)(2,1)}), bf16[192,768]{1,0:T(8,128)(2,1)}) %reduce-scatter.7.cloned.1.call-update) | async-done | bytes 294928 | tf_op jit(solution)/shard_map/reduce_scatter | solution.py:241
  410.1 60.1 %reduce-scatter.9.cloned.1.call-done = bf16[192,3072]{1,0:T(8,128)(2,1)} async-done(((bf16[768,3072]{1,0:T(8,128)(2,1)}), bf16[192,3072]{1,0:T(8,128)(2,1)}) %reduce-scatter.9.cloned.1.call-update) | async-done | bytes 1179664 | tf_op jit(solution)/shard_map/reduce_scatter | solution.py:241
  470.2 60.1 %reduce-scatter.11.cloned.1.call-done = bf16[768,768]{1,0:T(8,128)(2,1)} async-done(((bf16[3072,768]{1,0:T(8,128)(2,1)}), bf16[768,768]{1,0:T(8,128)(2,1)}) %reduce-scatter.11.cloned.1.call-update) | async-done | bytes 1179664 | tf_op jit(solution)/shard_map/reduce_scatter | solution.py:241
  530.6 15.4 %all-reduce.16 = (bf16[768]{0:T(1024)(128)(2,1)S(1)}, bf16[1536]{0:T(1024)(128)(2,1)S(1)}, bf16[768]{0:T(1024)(128)(2,1)S(1)}, bf16[768]{0:T(1024)(128)(2,1)S(1)...) all-reduce(bf16[768]{0:T(1024)(128)(2,1)S(1)} %dynamic-update-slice, ...), channel_id=1, replica_groups=mesh['replica'=4,'group'=8] {'replica'}, use_global_device_ids=true, to_apply=%add.5 | all-reduce | flops 9984 | bytes 39936
  546.5 15.2 %all-reduce.14 = (bf16[384]{0:T(512)(128)(2,1)S(1)}, bf16[192]{0:T(256)(128)(2,1)S(1)}, bf16[192]{0:T(256)(128)(2,1)S(1)}, bf16[192]{0:T(256)(128)(2,1)S(1)}, bf...) all-reduce(bf16[384]{0:T(512)(128)(2,1)S(1)} %dynamic-slice.7, ...), channel_id=1, replica_groups=mesh['replica'=4,'group'=8] {'group'}, use_global_device_ids=true, to_apply=%region_20.21 | all-reduce | flops 2304 | bytes 9216 | tf_op jit(solution)/shard_map/psum | solution.py:246
  568.1 8.8 %add_convert_fusion.2 = bf16[1024,768]{1,0:T(8,128)(2,1)} fusion(f32[1024,768]{1,0:T(8,128)S(1)} %copy-done.5, bf16[1024,2304]{0,1:T(8,128)(2,1)} %bitcast.156, bf16[768,2304]{1,0:T(8,128)(2,1)} %all-gather.7.cloned.1.call-done, f32[1024]{0:T(1024)S(1)} %copy-done.27), kind=kOutput, calls=%fused_computation.60 | convolution fusion | flops 3626237952 | bytes 12980224 | tf_op jit(solution)/shard_map/dot_general | solution.py:35
  576.9 48.4 %all-reduce.20.cloned.1.call-done = (bf16[192,2304]{0,1:T(8,128)(2,1)}, bf16[192,768]{1,0:T(8,128)(2,1)}, bf16[192,3072]{1,0:T(8,128)(2,1)}, bf16[768,768]{1,0:T(8,128)(2,1)}) async-done(((bf16[192,2304]{0,1:T(8,128)(2,1)}, bf16[192,768]{1,0:T(8,128)(2,1)}, bf16[192,3072]{1,0:T(8,128)(2,1)}, bf16[768,768]{1,0:T(8,128)(2,1)}), (bf16[192,2304]{0,1:T(8,128)(2,1)}, bf16[192,768]{1,0:T(8,128)(2,1)}, ...) | async-done | bytes 3538960 | tf_op jit(solution)/shard_map/psum | solution.py:246
  625.4 3.1 convert_element_type.243
  (248 shorter events, 64.6 us)
Async XLA Ops:
  7.2 4.7 copy-start.52
  7.2 5.0 copy-start.53
  7.2 5.2 copy-start.54
  7.2 23.2 %copy-start.44 = (bf16[384]{0:T(512)(128)(2,1)S(1)}, bf16[384]{0:T(512)(128)(2,1)}, u32[]{:S(2)}) copy-start(bf16[384]{0:T(512)(128)(2,1)} %param.24) | copy-start | bytes 2308
  7.3 30.3 %copy-start.55 = (s32[64]{0:T(128)S(1)}, s32[64]{0:T(128)}, u32[]{:S(2)}) copy-start(s32[64]{0:T(128)} %param.21) | copy-start | bytes 772
  7.3 30.3 %copy-start.56 = (s32[2]{0:T(128)S(1)}, s32[2]{0:T(128)}, u32[]{:S(2)}) copy-start(s32[2]{0:T(128)} %param.22) | copy-start | bytes 28
  7.3 32.3 %copy-start.43 = (bf16[768]{0:T(1024)(128)(2,1)S(1)}, bf16[768]{0:T(1024)(128)(2,1)}, u32[]{:S(2)}) copy-start(bf16[768]{0:T(1024)(128)(2,1)} %param.30) | copy-start | bytes 4612
  7.3 52.9 %copy-start.45 = (bf16[2,512,768]{2,1,0:T(8,128)(2,1)S(1)}, bf16[2,512,768]{2,1,0:T(8,128)(2,1)}, u32[]{:S(2)}) copy-start(bf16[2,512,768]{2,1,0:T(8,128)(2,1)} %param.20) | copy-start | bytes 4718596
  7.3 52.9 %all-gather.7.cloned.1.call-start = ((), (), s32[]{:S(2)}) async-start(), calls=%async_computation.4 | async-start | bytes 4423680 | tf_op jit(solution)/shard_map/all_gather | solution.py:72
  8.0 103.8 %all-gather.9.cloned.1.call-start = ((), (), s32[]{:S(2)}) async-start(), calls=%async_computation.5 | async-start | bytes 1474560 | tf_op jit(solution)/shard_map/all_gather | solution.py:74
  8.8 139.9 %all-gather.11.cloned.1.call-start = ((), (), s32[]{:S(2)}) async-start(), calls=%async_computation.6 | async-start | bytes 5898240 | tf_op jit(solution)/shard_map/all_gather | solution.py:129
  9.5 198.0 %all-gather.13.cloned.1.call-start = ((), (), s32[]{:S(2)}) async-start(), calls=%async_computation.7 | async-start | bytes 5898240 | tf_op jit(solution)/shard_map/all_gather | solution.py:131
  10.1 368.1 %reduce-scatter.13.cloned.1.call-start = ((), (), s32[]{:S(2)}) async-start(), calls=%async_computation.11 | async-start | bytes 4423680
  83.2 5.6 copy-start.47
  116.7 128.9 %copy-start.6 = (f32[1024,768]{1,0:T(8,128)}, f32[1024,768]{1,0:T(8,128)S(1)}, u32[]{:S(2)}) copy-start(f32[1024,768]{1,0:T(8,128)S(1)} %get-tuple-element.252) | copy-start | bytes 9437188
  116.7 32.0 %copy-start.28 = (f32[768]{0:T(1024)S(1)}, f32[768]{0:T(1024)}, u32[]{:S(2)}) copy-start(f32[768]{0:T(1024)} %convert_element_type.212) | copy-start | bytes 9220
  116.7 32.0 %copy-start.32 = (f32[4,1,768]{2,1,0:T(1,128)S(1)}, f32[4,1,768]{2,1,0:T(1,128)}, u32[]{:S(2)}) copy-start(f32[4,1,768]{2,1,0:T(1,128)} %convert_element_type.257) | copy-start | bytes 36868
  116.7 31.9 %copy-start.37 = (f32[768]{0:T(1024)S(1)}, f32[768]{0:T(1024)}, u32[]{:S(2)}) copy-start(f32[768]{0:T(1024)} %convert_element_type.213) | copy-start | bytes 9220
  116.8 128.8 %copy-start.23 = (f32[1024]{0:T(1024)}, f32[1024]{0:T(1024)S(1)}, u32[]{:S(2)}) copy-start(f32[1024]{0:T(1024)S(1)} %broadcast_multiply_fusion.1) | copy-start | bytes 12292
  117.3 128.3 %copy-start.30 = (f32[1024]{0:T(1024)}, f32[1024]{0:T(1024)S(1)}, u32[]{:S(2)}) copy-start(f32[1024]{0:T(1024)S(1)} %fusion.32) | copy-start | bytes 12292
  148.7 58.8 %copy-start.39 = (f32[768]{0:T(1024)S(1)}, f32[768]{0:T(1024)}, u32[]{:S(2)}) copy-start(f32[768]{0:T(1024)} %convert_element_type.217) | copy-start | bytes 9220
  216.3 4.7 copy-start
  216.3 4.7 copy-start.15
  216.9 5.9 copy-start.21
  222.8 16.2 %slice-start = ((s8[4718592]{0:T(1024)(128)(4,1)}), s8[4194304]{0:T(1024)(128)(4,1)S(1)}, s32[]{:S(2)}) async-start(s8[4718592]{0:T(1024)(128)(4,1)} %bitcast.163), calls=%async_computation.13 | async-start | bytes 8388608
  223.7 15.3 %copy-start.9 = (bf16[1024,768]{1,0:T(8,128)(2,1)}, bf16[1024,768]{1,0:T(8,128)(2,1)S(1)}, u32[]{:S(2)}) copy-start(bf16[1024,768]{1,0:T(8,128)(2,1)S(1)} %get-tuple-element.233) | copy-start | bytes 4718596
  223.7 15.3 %slice-start.1 = ((s8[4718592]{0:T(1024)(128)(4,1)}), s8[524288]{0:T(1024)(128)(4,1)S(1)}, s32[]{:S(2)}) async-start(s8[4718592]{0:T(1024)(128)(4,1)} %bitcast.163), calls=%async_computation.14 | async-start | bytes 1048576
  239.0 6.6 %copy-start.58 = (bf16[1024,3072]{1,0:T(8,128)(2,1)}, bf16[1024,3072]{1,0:T(8,128)(2,1)S(1)}, u32[]{:S(2)}) copy-start(bf16[1024,3072]{1,0:T(8,128)(2,1)S(1)} %get-tuple-element.259) | copy-start | bytes 18874372
  316.5 6.1 copy-start.46
  330.8 4.7 copy-start.7
  330.8 79.2 %reduce-scatter.7.cloned.1.call-start = ((), (), s32[]{:S(2)}) async-start(), calls=%async_computation.8 | async-start | bytes 1474560 | tf_op jit(solution)/shard_map/reduce_scatter | solution.py:241
  335.4 134.8 %reduce-scatter.9.cloned.1.call-start = ((), (), s32[]{:S(2)}) async-start(), calls=%async_computation.9 | async-start | bytes 5898240 | tf_op jit(solution)/shard_map/reduce_scatter | solution.py:241
  346.3 184.0 %reduce-scatter.11.cloned.1.call-start = ((), (), s32[]{:S(2)}) async-start(), calls=%async_computation.10 | async-start | bytes 5898240 | tf_op jit(solution)/shard_map/reduce_scatter | solution.py:241
  357.6 267.8 %all-reduce.20.cloned.1.call-start = ((), (), s32[]{:S(2)}) async-start(), calls=%async_computation.12 | async-start | bytes 7667712 | tf_op jit(solution)/shard_map/psum | solution.py:246
  363.4 167.1 %copy-start.33 = (bf16[768]{0:T(1024)(128)(2,1)S(1)}, bf16[768]{0:T(1024)(128)(2,1)}, u32[]{:S(2)}) copy-start(bf16[768]{0:T(1024)(128)(2,1)} %get-tuple-element.179) | copy-start | bytes 4612
  363.4 167.1 %copy-start.34 = (bf16[768]{0:T(1024)(128)(2,1)S(1)}, bf16[768]{0:T(1024)(128)(2,1)}, u32[]{:S(2)}) copy-start(bf16[768]{0:T(1024)(128)(2,1)} %get-tuple-element.232) | copy-start | bytes 4612
  363.4 167.1 %copy-start.35 = (bf16[768]{0:T(1024)(128)(2,1)S(1)}, bf16[768]{0:T(1024)(128)(2,1)}, u32[]{:S(2)}) copy-start(bf16[768]{0:T(1024)(128)(2,1)} %get-tuple-element.234) | copy-start | bytes 4612
  363.4 167.1 %copy-start.36 = (bf16[3072]{0:T(1024)(128)(2,1)S(1)}, bf16[3072]{0:T(1024)(128)(2,1)}, u32[]{:S(2)}) copy-start(bf16[3072]{0:T(1024)(128)(2,1)} %get-tuple-element.258) | copy-start | bytes 18436
  363.4 167.1 %copy-start.40 = (bf16[768]{0:T(1024)(128)(2,1)S(1)}, bf16[768]{0:T(1024)(128)(2,1)}, u32[]{:S(2)}) copy-start(bf16[768]{0:T(1024)(128)(2,1)} %get-tuple-element.177) | copy-start | bytes 4612
  363.5 167.1 %copy-start.41 = (bf16[768]{0:T(1024)(128)(2,1)S(1)}, bf16[768]{0:T(1024)(128)(2,1)}, u32[]{:S(2)}) copy-start(bf16[768]{0:T(1024)(128)(2,1)} %get-tuple-element.181) | copy-start | bytes 4612
  363.5 202.9 %copy-start.1 = (f32[1024,768]{1,0:T(8,128)S(1)}, f32[1024,768]{1,0:T(8,128)}, u32[]{:S(2)}) copy-start(f32[1024,768]{1,0:T(8,128)} %copy-done) | copy-start | bytes 9437188
  363.5 202.9 %copy-start.16 = (f32[1024]{0:T(1024)S(1)}, f32[1024]{0:T(1024)}, u32[]{:S(2)}) copy-start(f32[1024]{0:T(1024)} %copy-done.15) | copy-start | bytes 12292
  363.5 202.9 %copy-start.18 = (f32[768]{0:T(1024)S(1)}, f32[768]{0:T(1024)}, u32[]{:S(2)}) copy-start(f32[768]{0:T(1024)} %convert_element_type.218) | copy-start | bytes 9220
  363.5 202.9 %copy-start.20 = (f32[1,4,2,128]{3,1,2,0:T(4,128)S(1)}, f32[1,4,2,128]{3,1,2,0:T(4,128)}, u32[]{:S(2)}) copy-start(f32[1,4,2,128]{3,1,2,0:T(4,128)} %copy.86) | copy-start | bytes 12292
  363.5 202.9 %copy-start.22 = (f32[1024]{0:T(1024)S(1)}, f32[1024]{0:T(1024)}, u32[]{:S(2)}) copy-start(f32[1024]{0:T(1024)} %copy-done.21) | copy-start | bytes 12292
  530.3 37.8 %copy-start.27 = (f32[1024]{0:T(1024)S(1)}, f32[1024]{0:T(1024)}, u32[]{:S(2)}) copy-start(f32[1024]{0:T(1024)} %copy-done.26) | copy-start | bytes 12292
  561.8 6.3 copy-start.5
  625.4 4.7 copy-start.13
  (24 other events, 70.5 us)
Sparse Core Ops, SparseCore 0:
  10.0 50.1 all-gather.6
  62.0 27.6 all-gather.8
  91.6 57.0 all-gather.10
  150.4 57.0 all-gather.12
  330.9 47.2 reduce-scatter.12
  381.5 28.5 reduce-scatter.6
  413.0 57.0 reduce-scatter.8
  473.2 57.0 reduce-scatter.10
  533.5 91.8 all-reduce.19
where the time goes:
time: 645 us; the launch traced here: 639 us
  waiting for transfers between devices  303 us (47%)
  matrix products  135 us (21%)
  local copies, waits for them, and re-layouts  68.8 us (11%)
  blocking collectives  63.7 us (10%)
  other arithmetic  50.2 us (8%)
  between operations  17.9 us (3%)
    reduce_scatter x3, waiting for transfers between devices, body(): lax.psum_scatter(as_sent(attn_terms + mlp_terms), 'replica', scatter_dime...  150 us
    psum x1, waiting for transfers between devices, body(): lax.psum(as_sent(shares), 'group')  48.4 us
    all_gather x1, waiting for transfers between devices, body(): lax.all_gather(down_weight, 'replica', axis=0, tiled=True)  46.2 us
    unnamed x2, blocking collectives  33.1 us
    dot_general x4, matrix products, back_product(): lax.dot_general(grad_rows, weight, (((1,), (1,)), ((), ())), preferred_el...  32 us
    all_gather x1, waiting for transfers between devices, body(): lax.all_gather(up_weight, 'replica', axis=0, tiled=True)  31.4 us
    dot_general x4, matrix products, weight_grad(): lax.dot_general(left, right, (((0,), (0,)), ((), ())), preferred_element_...  29.2 us
    unnamed x154, local copies, waits for them, and re-layouts  24.7 us
  transfers between devices with their start and end apart: 9, of which 8 were waited for; matrix products, arithmetic and copies ran while one was open for 19% of the time, Pallas kernels for 0%

commit v1 on v0

v1 whole, which is shorter than its diff:
```python
import jax
import jax.numpy as jnp
from jax import lax
from jax.experimental import pallas as pl
from jax.experimental.pallas import tpu as pltpu
from jax.sharding import Mesh
from jax.sharding import PartitionSpec as P

HEADS = 12
LANES = 128
NT = (((1,), (1,)), ((), ()))
NN = (((1,), (0,)), ((), ()))
TN = (((0,), (0,)), ((), ()))


def dot(left, right, dims):
    return lax.dot_general(left, right, dims, preferred_element_type=jnp.float32)


def layer_norm(row_data, gain_row, shift_row):
    row_mean = jnp.mean(row_data, axis=-1, keepdims=True)
    centred = row_data - row_mean
    spread = jnp.mean(centred * centred, axis=-1, keepdims=True)
    return centred * lax.rsqrt(spread + 1e-06) * gain_row + shift_row


def gelu_exact(values):
    return 0.5 * values * (1.0 + lax.erf(values * 0.7071067811865476))


def column_sum(grad_rows):
    return jnp.sum(grad_rows.astype(jnp.float32), axis=0)


def attend_kernel(lens_ref, qkv_ref, ctx_ref, lse_ref, *, width, head_size):
    seqlen = qkv_ref.shape[0]
    valid = lax.broadcasted_iota(jnp.int32, (seqlen, seqlen), 0) < lens_ref[pl.program_id(0)]
    scale = head_size ** (-0.5)
    per = LANES // head_size
    for pair in range(width // LANES):
        at = pair * LANES
        queries = qkv_ref[:, at : at + LANES] * jnp.asarray(scale, jnp.bfloat16)
        key_rows = qkv_ref[:, width + at : width + at + LANES]
        values = qkv_ref[:, 2 * width + at : 2 * width + at + LANES]
        parts = []
        for sub in range(per):
            cut = slice(sub * head_size, (sub + 1) * head_size)
            scores = dot(key_rows[:, cut], queries[:, cut], NT)
            scores = jnp.where(valid, scores, -1e30)
            top = jnp.max(scores, axis=0, keepdims=True)
            grown = jnp.exp(scores - top)
            total = jnp.sum(grown, axis=0, keepdims=True)
            soft = (grown * (1.0 / total)).astype(jnp.bfloat16)
            parts.append(dot(soft, values[:, cut], TN))
            lse_ref[0, pair * per + sub : pair * per + sub + 1, :] = top + jnp.log(total)
        ctx_ref[:, at : at + LANES] = jnp.concatenate(parts, axis=1).astype(jnp.bfloat16)


def attend_back_kernel(lens_ref, qkv_ref, lse_ref, dctx_ref, dqkv_ref, *, width, head_size):
    seqlen = qkv_ref.shape[0]
    valid = lax.broadcasted_iota(jnp.int32, (seqlen, seqlen), 0) < lens_ref[pl.program_id(0)]
    scale = head_size ** (-0.5)
    per = LANES // head_size
    for pair in range(width // LANES):
        at = pair * LANES
        queries = qkv_ref[:, at : at + LANES] * jnp.asarray(scale, jnp.bfloat16)
        key_rows = qkv_ref[:, width + at : width + at + LANES]
        values = qkv_ref[:, 2 * width + at : 2 * width + at + LANES]
        dctx = dctx_ref[:, at : at + LANES]
        dq, dk, dv = [], [], []
        for sub in range(per):
            cut = slice(sub * head_size, (sub + 1) * head_size)
            scores = dot(key_rows[:, cut], queries[:, cut], NT)
            lse = lse_ref[0, pair * per + sub : pair * per + sub + 1, :]
            soft = jnp.where(valid, jnp.exp(scores - lse), 0.0)
            dsoft = dot(values[:, cut], dctx[:, cut], NT)
            dv.append(dot(soft.astype(jnp.bfloat16), dctx[:, cut], NN))
            inner = jnp.sum(soft * dsoft, axis=0, keepdims=True)
            dscores = (soft * (dsoft - inner)).astype(jnp.bfloat16)
            dq.append(dot(dscores, key_rows[:, cut], TN) * scale)
            dk.append(dot(dscores, queries[:, cut], NN))
        for place, part in enumerate((dq, dk, dv)):
            start = place * width + at
            dqkv_ref[:, start : start + LANES] = jnp.concatenate(part, axis=1).astype(jnp.bfloat16)


def attend(slot_lens, projected, slot_count, head_count):
    rows, wide = projected.shape
    seqlen, width = rows // slot_count, wide // 3
    head_size = width // head_count
    return pl.pallas_call(
        lambda *refs: attend_kernel(*refs, width=width, head_size=head_size),
        grid_spec=pltpu.PrefetchScalarGridSpec(
            num_scalar_prefetch=1,
            grid=(slot_count,),
            in_specs=[pl.BlockSpec((seqlen, wide), lambda i, lens: (i, 0))],
            out_specs=[
                pl.BlockSpec((seqlen, width), lambda i, lens: (i, 0)),
                pl.BlockSpec((1, head_count, seqlen), lambda i, lens: (i, 0, 0)),
            ],
        ),
        out_shape=[
            jax.ShapeDtypeStruct((rows, width), jnp.bfloat16),
            jax.ShapeDtypeStruct((slot_count, head_count, seqlen), jnp.float32),
        ],
        compiler_params=pltpu.CompilerParams(vmem_limit_bytes=48 * 2**20),
        cost_estimate=pl.CostEstimate(
            flops=4 * rows * seqlen * width * 4,
            bytes_accessed=8 * rows * width,
            transcendentals=rows * seqlen * head_count,
        ),
        name="attend",
    )(slot_lens, projected)


def attend_back(slot_lens, projected, lse, dctx, slot_count, head_count):
    rows, wide = projected.shape
    seqlen, width = rows // slot_count, wide // 3
    head_size = width // head_count
    return pl.pallas_call(
        lambda *refs: attend_back_kernel(*refs, width=width, head_size=head_size),
        grid_spec=pltpu.PrefetchScalarGridSpec(
            num_scalar_prefetch=1,
            grid=(slot_count,),
            in_specs=[
                pl.BlockSpec((seqlen, wide), lambda i, lens: (i, 0)),
                pl.BlockSpec((1, head_count, seqlen), lambda i, lens: (i, 0, 0)),
                pl.BlockSpec((seqlen, width), lambda i, lens: (i, 0)),
            ],
            out_specs=pl.BlockSpec((seqlen, wide), lambda i, lens: (i, 0)),
        ),
        out_shape=jax.ShapeDtypeStruct((rows, wide), jnp.bfloat16),
        compiler_params=pltpu.CompilerParams(vmem_limit_bytes=48 * 2**20),
        cost_estimate=pl.CostEstimate(
            flops=10 * rows * seqlen * width * 4,
            bytes_accessed=14 * rows * width,
            transcendentals=rows * seqlen * head_count,
        ),
        name="attend_back",
    )(slot_lens, projected, lse, dctx)


def hop(part, axis, mask):
    pairs = [(place, place ^ mask) for place in range(lax.axis_size(axis))]
    return lax.ppermute(part, axis, pairs)


def take(parts, index):
    return lax.dynamic_index_in_dim(parts, index, 0, keepdims=False)


def add(left, right):
    return left.astype(jnp.float32) + right.astype(jnp.float32)


def low(part):
    return part.astype(jnp.bfloat16)


def gather_start(shard):
    rows, cols = shard.shape
    halves = shard.reshape(2, 2, rows // 4, cols)
    mine = take(halves, lax.axis_index("core"))
    first = hop(mine, "replica", 1)
    second = hop(mine, "replica", 2)
    return first, second


def gather_end(shard, first, second):
    rows, cols = shard.shape
    me, core = lax.axis_index("replica"), lax.axis_index("core")
    third = jnp.stack([hop(first[0], "replica", 2), hop(second[1], "replica", 1)])
    halves = shard.reshape(2, 2, rows // 4, cols)
    mine = [first, second, third]
    theirs = [hop(part, "core", 1) for part in mine]
    blocks = [halves]
    for own, other in zip(mine, theirs):
        low_half = jnp.where(core == 0, own, other)
        high_half = jnp.where(core == 0, other, own)
        blocks.append(jnp.stack([low_half, high_half]))
    full = jnp.stack(blocks)
    return jnp.concatenate([take(full, me ^ owner) for owner in range(4)], axis=0).reshape(
        4 * rows, cols
    )


def gather_small(row):
    me = lax.axis_index("replica")
    near = jnp.stack([row, hop(row, "replica", 1)])
    full = jnp.concatenate([near, hop(near, "replica", 2)], axis=0)
    return jnp.stack([take(full, me ^ owner) for owner in range(4)])


def sum_small(rows):
    for axis in ("core", "replica", "chain"):
        mask = 1
        while mask < lax.axis_size(axis):
            rows = rows + hop(rows, axis, mask)
            mask *= 2
    return rows


def share(grad):
    rows, cols = grad.shape
    me, core = lax.axis_index("replica"), lax.axis_index("core")
    place, depth = lax.axis_index("chain"), lax.axis_size("chain")
    pieces = low(grad).reshape(4, 2, 2, rows // 16, cols)
    own = lax.dynamic_index_in_dim(pieces, core, 1, keepdims=False)
    other = lax.dynamic_index_in_dim(pieces, 1 - core, 1, keepdims=False)
    part = low(add(own, hop(other, "core", 1)))
    front, back = part[:, 0], part[:, 1]
    got_front = hop(jnp.stack([take(front, me ^ 1), take(front, me ^ 3)]), "replica", 1)
    got_back = hop(jnp.stack([take(back, me ^ 2), take(back, me ^ 3)]), "replica", 2)
    far_front = hop(low(add(take(front, me ^ 2), got_front[1])), "replica", 2)
    far_back = hop(low(add(take(back, me ^ 1), got_back[1])), "replica", 1)
    total = jnp.concatenate(
        [
            add(add(take(front, me), got_front[0]), far_front),
            add(add(take(back, me), got_back[0]), far_back),
        ],
        axis=0,
    )
    total = low(total)
    mask = 1
    while mask < depth:
        bit = (place // mask) % 2
        split = total.reshape(2, total.shape[0] // 2, cols)
        total = low(add(take(split, bit), hop(take(split, 1 - bit), "chain", mask)))
        mask *= 2
    while mask > 1:
        mask //= 2
        bit = (place // mask) % 2
        other = hop(total, "chain", mask)
        total = jnp.concatenate(
            [jnp.where(bit == 0, total, other), jnp.where(bit == 0, other, total)], axis=0
        )
    other = hop(total, "core", 1)
    return jnp.concatenate(
        [jnp.where(core == 0, total, other), jnp.where(core == 0, other, total)], axis=0
    ).astype(jnp.float32)


def body(
    tokens,
    lengths,
    slot_order,
    qkv_weight,
    qv_bias,
    out_weight,
    out_bias,
    attn_gain,
    attn_shift,
    up_weight,
    up_bias,
    down_weight,
    down_bias,
    mlp_gain,
    mlp_shift,
    cotangent,
):
    slot_count, seqlen, width = tokens.shape
    row_count = slot_count * seqlen
    owners = lax.axis_size("replica")
    picked = slot_order[:, None] == jnp.arange(lengths.shape[0], dtype=jnp.int32)[None, :]
    slot_lens = jnp.sum(jnp.where(picked, lengths[None, :], 0), axis=1)
    valid_rows = jnp.arange(seqlen, dtype=jnp.int32)[None, :] < slot_lens[:, None]
    row_valid = valid_rows.reshape(row_count, 1).astype(jnp.float32)

    small = (qv_bias, out_bias, attn_gain, attn_shift, up_bias, down_bias, mlp_gain, mlp_shift)
    sizes = [part.shape[0] for part in small]
    packed = gather_small(jnp.concatenate(small))
    full_small, at = [], 0
    for size in sizes:
        full_small.append(packed[:, at : at + size].reshape(owners * size).astype(jnp.float32))
        at += size
    qv, outb, gain1, shift1, upb, downb, gain2, shift2 = full_small
    first, second = gather_start(qkv_weight)
    full_qkv = gather_end(qkv_weight, first, second)
    first, out_shard, up_shard, down_shard = lax.optimization_barrier(
        (first, out_weight, up_weight, down_weight)
    )
    full_out = gather_end(out_shard, *gather_start(out_shard))
    full_up = gather_end(up_shard, *gather_start(up_shard))
    full_down = gather_end(down_shard, *gather_start(down_shard))

    flat = tokens.reshape(row_count, width)
    bias_row = jnp.concatenate([qv[:width], jnp.zeros((width,), jnp.float32), qv[width:]])
    projected = (dot(flat, full_qkv, NN) + bias_row).astype(jnp.bfloat16)
    ctx, lse = attend(slot_lens, projected, slot_count, HEADS)
    res1 = flat.astype(jnp.float32) + dot(ctx, full_out, NN) + outb
    hidden = layer_norm(res1, gain1, shift1)
    hidden_low = hidden.astype(jnp.bfloat16)
    pre_act = dot(hidden_low, full_up, NN) + upb
    activ_low = gelu_exact(pre_act).astype(jnp.bfloat16)
    res2 = hidden + dot(activ_low, full_down, NN) + downb
    normed = layer_norm(res2, gain2, shift2)
    layer_out = (normed * row_valid).astype(jnp.bfloat16).reshape(slot_count, seqlen, width)

    grad_out = cotangent.reshape(row_count, width).astype(jnp.float32) * row_valid
    unused_second, second_pull = jax.vjp(layer_norm, res2, gain2, shift2)
    dres2, grad_gain2, grad_shift2 = second_pull(grad_out)
    ddown = dres2.astype(jnp.bfloat16)
    grad_down = share(dot(activ_low, ddown, TN))
    dactiv = dot(ddown, full_down, NT)
    unused_act, gelu_pull = jax.vjp(gelu_exact, pre_act)
    dpre = gelu_pull(dactiv)[0].astype(jnp.bfloat16)
    grad_up = share(dot(hidden_low, dpre, TN))
    dhidden = dres2 + dot(dpre, full_up, NT)
    unused_first, first_pull = jax.vjp(layer_norm, res1, gain1, shift1)
    dres1, grad_gain1, grad_shift1 = first_pull(dhidden)
    dattn = dres1.astype(jnp.bfloat16)
    grad_out_weight = share(dot(ctx, dattn, TN))
    dctx = dot(dattn, full_out, NT).astype(jnp.bfloat16)
    dqkv = attend_back(slot_lens, projected, lse, dctx, slot_count, HEADS)
    grad_qkv = share(dot(flat, dqkv, TN))
    proj_sums = column_sum(dqkv)
    grad_tokens = (dres1 + dot(dqkv, full_qkv, NT)).astype(jnp.bfloat16)
    grad_tokens = grad_tokens.reshape(slot_count, seqlen, width)

    small_grads = (
        jnp.concatenate([proj_sums[:width], proj_sums[2 * width :]]),
        column_sum(dattn),
        grad_gain1,
        grad_shift1,
        column_sum(dpre),
        column_sum(ddown),
        grad_gain2,
        grad_shift2,
    )
    together = jnp.concatenate([part.reshape(owners, -1) for part in small_grads], axis=1)
    summed = sum_small(together)
    own = lax.dynamic_slice_in_dim(summed, lax.axis_index("replica"), 1, 0)[0]
    shares, at = [], 0
    for size in sizes:
        shares.append(own[at : at + size])
        at += size
    return (
        layer_out,
        grad_tokens,
        grad_qkv,
        shares[0],
        grad_out_weight,
        shares[1],
        shares[2],
        shares[3],
        grad_up,
        shares[4],
        grad_down,
        shares[5],
        shares[6],
        shares[7],
    )


def solution(mesh):
    owners, sharers = mesh.devices.shape
    split = Mesh(mesh.devices.reshape(owners, sharers // 2, 2), ("replica", "chain", "core"))
    rows = P(("replica", "chain", "core"), None, None)
    flat = P("replica")
    wide = P("replica", None)
    weights = (wide, flat, wide, flat, flat, flat, wide, flat, wide, flat, flat, flat)
    return jax.shard_map(
        body,
        mesh=split,
        in_specs=(rows, P(), P(("replica", "chain", "core"))) + weights + (rows,),
        out_specs=(rows, rows) + weights,
        check_vma=False,
    )
```

time: 645 us -> 388 us (0.60)
  waiting for transfers between devices: 303 us -> 106 us
  starting transfers between devices: 0.36 us -> 83.2 us
  blocking collectives: 63.7 us -> 0 us
  matrix products: 135 us -> 81.5 us
  Pallas kernels: 0 us -> 37.6 us
  local copies, waits for them, and re-layouts: 68.8 us -> 32.9 us
  between operations: 17.9 us -> 2.23 us
  other arithmetic: 50.2 us -> 38.2 us
    reduce_scatter x3 -> x0, waiting for transfers between devices: 150 us -> none  [body(): lax.psum_scatter(as_sent(attn_terms + mlp_terms), 'replica', scatter_dime...]
    ppermute x0 -> x75, waiting for transfers between devices: none -> 106 us  [hop(): return lax.ppermute(part, axis, pairs)]
    all_gather x4 -> x0, waiting for transfers between devices: 87.4 us -> none  [the longest x1 46.2 us: body(): lax.all_gather(down_weight, 'replica', axis=0, tiled=True)]
    ppermute x0 -> x75, starting transfers between devices: none -> 83.2 us  [hop(): return lax.ppermute(part, axis, pairs)]
    dot_general x26 -> x12, matrix products: 135 us -> 81.5 us  [dot(): lax.dot_general(left, right, dims, preferred_element_type=jnp.float32)]
    psum x1 -> x0, waiting for transfers between devices: 48.4 us -> none  [body(): lax.psum(as_sent(shares), 'group')]
    pallas_call x0 -> x2, Pallas kernels: none -> 37.6 us  [the longest x1 25 us: attend_back(): pl.pallas_call(lambda *refs: attend_back_kernel(*refs, width=width, head_...]
    unnamed x2 -> x0, blocking collectives: 33.1 us -> none
  transfers between devices with their start and end apart: 9 -> 75, of which waited for: 8 -> 42; matrix products, arithmetic and copies ran while one was open for 19% -> 17% of each run, Pallas kernels for 0% -> 3%
where the time goes in v1:
time: 388 us; the launch traced here: 382 us
  waiting for transfers between devices  106 us (27%)
  starting transfers between devices  83.2 us (21%)
  matrix products  81.5 us (21%)
  other arithmetic  38.2 us (10%)
  Pallas kernels  37.6 us (10%)
  local copies, waits for them, and re-layouts  32.9 us (8%)
    ppermute x75, waiting for transfers between devices, hop(): return lax.ppermute(part, axis, pairs)  106 us
    ppermute x75, starting transfers between devices, hop(): return lax.ppermute(part, axis, pairs)  83.2 us
    dot_general x12, matrix products, dot(): lax.dot_general(left, right, dims, preferred_element_type=jnp.float32)  81.5 us
    pallas_call x1, Pallas kernels, attend_back(): pl.pallas_call(lambda *refs: attend_back_kernel(*refs, width=width, head_...  25 us
    pallas_call x1, Pallas kernels, attend(): pl.pallas_call(lambda *refs: attend_kernel(*refs, width=width, head_size=...  12.6 us
  transfers between devices with their start and end apart: 75, of which 42 were waited for; matrix products, arithmetic and copies ran while one was open for 17% of the time, Pallas kernels for 3%

profile of v1, /device:TPU:0, one launch (start us, length us, event | category | flops | bytes accessed | tf_op | source)
XLA Modules:
  0.0 382.0 jit_solution(18084469559038105163)
XLA Ops:
  0.7 2.0 dynamic-slice_bitcast_fusion.18
  2.6 2.9 collective-permute-start
  7.1 6.1 %concatenate.82 = bf16[2304]{0:T(1024)(128)(2,1)} concatenate(bf16[384]{0:T(512)(128)(2,1)} %param.20, bf16[192]{0:T(256)(128)(2,1)} %param.22, bf16[192]{0:T(256)(128)(2,1)} %param.23, bf16[192]{0:T(256)(128)(2,1)} %param.24, bf16[768]{0:T(1024)(128)(2,1)} %param.26, bf16[192]{0:T(256)(128)(2,1)} %param.28, bf16[192]{0:T(256)(128)(2,1)} %param.29, bf16[192]{0:T(256)(128)(2,1)} %param.30), dimensions={0} | concatenate | bytes 9216 | tf_op jit(solution)/shard_map/concatenate | solution.py:271
  19.1 2.4 multiply_reduce_fusion
  46.2 11.6 %collective-permute-done.9 = bf16[2,48,768]{2,1,0:T(8,128)(2,1)S(1)} collective-permute-done((bf16[2,48,768]{2,1,0:T(8,128)(2,1)S(1)}, bf16[2,48,768]{2,1,0:T(8,128)(2,1)S(1)}, u32[]{:S(2)}, u32[]{:S(2)}) %collective-permute-start.9) | collective-permute-done | bytes 147488 | tf_op jit(solution)/shard_map/ppermute | solution.py:145
  59.3 2.3 collective-permute-done.11
  62.2 2.4 collective-permute-done.4
  66.7 2.8 collective-permute-done.14
  78.5 3.3 collective-permute-done.16
  82.6 2.0 collective-permute-done.18
  88.0 5.4 %fusion.refs_1_ = bf16[1024,2304]{1,0:T(8,128)(2,1)} fusion(bf16[1024,768]{1,0:T(8,128)(2,1)S(1)} %bitcast.500, bf16[768,2304]{1,0:T(8,128)(2,1)S(1)} %bitcast.441, f32[2304]{0:T(1024)S(1)} %pad_maximum_fusion.34), kind=kOutput, calls=%fused_computation.9 | convolution fusion | flops 3628597248 | bytes 9839616 | tf_op jit(solution)/shard_map/dot_general | solution.py:17
  93.4 12.6 %attend.1 = (bf16[1024,768]{1,0:T(8,128)(2,1)S(1)}, f32[2,12,512]{2,1,0:T(8,128)S(1)}) custom-call(s32[2]{0:T(128)S(1)} %fusion.42.refs_0_, bf16[1024,2304]{1,0:T(8,128)(2,1)} %fusion.refs_1_), custom_call_target="tpu_custom_call" | custom-call | flops 6442450944 | bytes 6291456 | tf_op jit(solution)/shard_map/attend/pallas_call | solution.py:91
  106.1 2.9 fusion.56
  118.6 11.3 %multiply_convert_fusion = (bf16[1024,3072]{1,0:T(8,128)(2,1)}, f32[1024,3072]{1,0:T(8,128)}) fusion(f32[3072]{0:T(1024)S(1)} %copy-done.16, bf16[768,3072]{1,0:T(8,128)(2,1)S(1)} %bitcast.437, f32[1024,768]{1,0:T(8,128)S(1)} %get-tuple-element.149, f32[768]{0:T(1024)S(1)} %reshape.463, f32[768]{0:T(1024)S(1)} %copy-done.14, f32[1024]{0:T(1024)S(1)} %fusion.40, ...), kind=kOutput, calls=%fused_computation.2 | convolution fusion | flops 4854644736 | bytes 26765312 | tf_op jit(solution)/shard_map/dot_general | solution.py:17
  130.0 7.6 %fusion.57 = (f32[1024]{0:T(1024)S(1)}, f32[1024,768]{1,0:T(8,128)S(1)}) fusion(f32[768]{0:T(1024)S(1)} %copy-done.17, bf16[1024,3072]{1,0:T(8,128)(2,1)} %get-tuple-element.150, bf16[3072,768]{1,0:T(8,128)(2,1)S(1)} %bitcast.439, f32[768]{0:T(1024)S(1)} %reshape.463, f32[768]{0:T(1024)S(1)} %copy-done.14, f32[1024]{0:T(1024)S(1)} %fusion.40, ...), kind=kOutput, calls=%fused_computation.313 | convolution fusion | flops 4837342208 | bytes 17323008 | tf_op jit(solution)/shard_map/dot_general | solution.py:17
  140.6 2.8 fusion.48
  144.0 7.0 %convolution_convert_fusion = bf16[3072,768]{1,0:T(8,128)(2,1)} fusion(bf16[1024,3072]{1,0:T(8,128)(2,1)S(1)} %bitcast.503, bf16[1024,768]{1,0:T(8,128)(2,1)S(1)} %get-tuple-element.30), kind=kOutput, calls=%fused_computation.6 | convolution fusion | flops 4834197504 | bytes 12582912 | tf_op jit(solution)/shard_map/dot_general | solution.py:17
  151.0 14.0 %convert_reduce_fusion = (f32[3072]{0:T(1024)S(1)}, bf16[1024,3072]{1,0:T(8,128)(2,1)}) fusion(bf16[1024,768]{1,0:T(8,128)(2,1)S(1)} %get-tuple-element.30, bf16[3072,768]{1,0:T(8,128)(2,1)S(1)} %bitcast.440, f32[1024,3072]{1,0:T(8,128)} %get-tuple-element.151, f32[3072]{0:T(1024)S(1)} %copy-done.16), kind=kOutput, calls=%fused_computation | convolution fusion | flops 4882166784 | bytes 25190400 | tf_op jit(solution)/shard_map/dot_general | solution.py:17
  165.0 10.1 %convolution_convert_fusion.1 = bf16[768,3072]{1,0:T(8,128)(2,1)} fusion(bf16[1024,3072]{1,0:T(8,128)(2,1)} %get-tuple-element.156, f32[1024,768]{1,0:T(8,128)S(1)} %get-tuple-element.149, f32[768]{0:T(1024)S(1)} %reshape.463, f32[768]{0:T(1024)S(1)} %copy-done.14, f32[1024]{0:T(1024)S(1)} %fusion.40, f32[1024]{0:T(1024)S(1)} %broadcast_multiply_fusion.1), kind=kOutput, calls=%fused_computation.7 | convolution fusion | flops 4838129664 | bytes 14170112 | tf_op jit(solution)/shard_map/dot_general | solution.py:17
  175.1 8.2 %multiply_reduce_fusion.2 = (f32[768]{0:T(1024)S(1)}, f32[1024]{0:T(1024)S(1)}, f32[768]{0:T(1024)S(1)}, f32[1024,768]{1,0:T(8,128)S(1)}) fusion(f32[1024,768]{1,0:T(8,128)S(1)} %get-tuple-element.149, f32[1024]{0:T(1024)S(1)} %fusion.40, f32[1024]{0:T(1024)S(1)} %broadcast_multiply_fusion.1, f32[768]{0:T(1024)S(1)} %copy-done.14, ...), kind=kOutput, calls=%fused_computation.28 | convolution fusion | flops 4839699456 | bytes 20472832 | tf_op jit(solution)/shard_map/dot_general | solution.py:17
  188.1 25.0 %attend_back.1 = bf16[1024,2304]{1,0:T(8,128)(2,1)} custom-call(s32[2]{0:T(128)S(1)} %fusion.42.refs_0_, bf16[1024,2304]{1,0:T(8,128)(2,1)} %fusion.refs_1_, f32[2,12,512]{2,1,0:T(8,128)S(1)} %get-tuple-element.23.refs_2_, bf16[1024,768]{1,0:T(8,128)(2,1)S(1)} %convolution_convert_fusion.3.refs_3_), custom_call_target="tpu_custom_call" | custom-call | flops 16106127360 | bytes 11010048 | tf_op jit(solution)/shard_map/attend_back/pallas_call | solution.py:120
  213.0 3.2 convert_reduce_fusion.1
  216.8 5.2 %add_convert_fusion.2 = bf16[1024,768]{1,0:T(8,128)(2,1)} fusion(f32[1024,768]{1,0:T(8,128)S(1)} %get-tuple-element.34, bf16[1024,2304]{1,0:T(8,128)(2,1)S(1)} %copy-done.1, bf16[768,2304]{1,0:T(8,128)(2,1)S(1)} %bitcast.442, f32[1024]{0:T(1024)S(1)} %negate_multiply_fusion), kind=kOutput, calls=%fused_computation.30 | convolution fusion | flops 3626237952 | bytes 12980224 | tf_op jit(solution)/shard_map/dot_general | solution.py:17
  223.3 6.8 %convolution_convert_fusion.2 = bf16[2304,768]{0,1:T(8,128)(2,1)S(1)} fusion(bf16[1024,2304]{1,0:T(8,128)(2,1)} %attend_back.1, bf16[1024,768]{1,0:T(8,128)(2,1)} %bitcast.499), kind=kOutput, calls=%fused_computation.8 | convolution fusion | flops 3625648128 | bytes 9830400 | tf_op jit(solution)/shard_map/dot_general | solution.py:17
  235.9 2.1 collective-permute-start.48
  238.0 2.1 collective-permute-done.46
  250.9 2.7 collective-permute-start.51
  255.8 2.9 collective-permute-start.52
  260.8 2.3 collective-permute-start.53
  270.9 10.2 %collective-permute-done.31 = bf16[2,48,2304]{2,1,0:T(8,128)(2,1)S(1)} collective-permute-done((bf16[2,48,2304]{2,1,0:T(8,128)(2,1)S(1)}, bf16[2,48,2304]{2,1,0:T(8,128)(2,1)S(1)}, u32[]{:S(2)}, u32[]{:S(2)}) %collective-permute-start.31) | collective-permute-done | bytes 442400 | tf_op jit(solution)/shard_map/ppermute | solution.py:145
  291.2 2.1 collective-permute-start.35
  294.3 2.9 collective-permute-done.35
  297.3 4.1 %collective-permute-start.36 = (bf16[24,2304]{1,0:T(8,128)(2,1)S(1)}, bf16[24,2304]{1,0:T(8,128)(2,1)S(1)}, u32[]{:S(2)}, u32[]{:S(2)}) collective-permute-start(bf16[24,2304]{1,0:T(8,128)(2,1)S(1)} %dynamic-slice_bitcast_fusion.41), channel_id=1, source_target_pairs={{0,4},{2,6},{4,0},{6,2},{1,5},{3,7},{5,1},{7,3},{8,12},{10,14},{12... | collective-permute-start | bytes 331784 | tf_op jit(solution)/shard_map/ppermute | solution.py:145
  301.4 5.5 %collective-permute-done.36 = bf16[24,2304]{1,0:T(8,128)(2,1)S(1)} collective-permute-done((bf16[24,2304]{1,0:T(8,128)(2,1)S(1)}, bf16[24,2304]{1,0:T(8,128)(2,1)S(1)}, u32[]{:S(2)}, u32[]{:S(2)}) %collective-permute-start.36) | collective-permute-done | bytes 110624 | tf_op jit(solution)/shard_map/ppermute | solution.py:145
  308.2 5.1 %collective-permute-done.37 = bf16[24,2304]{1,0:T(8,128)(2,1)S(1)} collective-permute-done((bf16[24,2304]{1,0:T(8,128)(2,1)S(1)}, bf16[24,2304]{1,0:T(8,128)(2,1)S(1)}, u32[]{:S(2)}, u32[]{:S(2)}) %collective-permute-start.37) | collective-permute-done | bytes 110624 | tf_op jit(solution)/shard_map/ppermute | solution.py:145
  318.4 4.6 %collective-permute-done.58 = bf16[2,48,3072]{2,1,0:T(8,128)(2,1)S(1)} collective-permute-done((bf16[2,48,3072]{2,1,0:T(8,128)(2,1)S(1)}, bf16[2,48,3072]{2,1,0:T(8,128)(2,1)S(1)}, u32[]{:S(2)}, u32[]{:S(2)}) %collective-permute-start.58) | collective-permute-done | bytes 589856 | tf_op jit(solution)/shard_map/ppermute | solution.py:145
  326.5 2.3 collective-permute-start.70
  330.1 2.3 collective-permute-start.60
  332.4 4.4 %collective-permute-done.70 = bf16[192,768]{1,0:T(8,128)(2,1)S(1)} collective-permute-done((bf16[192,768]{1,0:T(8,128)(2,1)S(1)}, bf16[192,768]{1,0:T(8,128)(2,1)S(1)}, u32[]{:S(2)}, u32[]{:S(2)}) %collective-permute-start.70) | collective-permute-done | bytes 294944 | tf_op jit(solution)/shard_map/ppermute | solution.py:145
  336.9 3.1 collective-permute-start.71
  340.0 4.4 %collective-permute-done.60 = bf16[48,3072]{1,0:T(8,128)(2,1)S(1)} collective-permute-done((bf16[48,3072]{1,0:T(8,128)(2,1)S(1)}, bf16[48,3072]{1,0:T(8,128)(2,1)S(1)}, u32[]{:S(2)}, u32[]{:S(2)}) %collective-permute-start.60) | collective-permute-done | bytes 294944 | tf_op jit(solution)/shard_map/ppermute | solution.py:145
  346.5 2.2 collective-permute-start.72
  348.7 6.0 %collective-permute-done.61 = bf16[24,3072]{1,0:T(8,128)(2,1)S(1)} collective-permute-done((bf16[24,3072]{1,0:T(8,128)(2,1)S(1)}, bf16[24,3072]{1,0:T(8,128)(2,1)S(1)}, u32[]{:S(2)}, u32[]{:S(2)}) %collective-permute-start.61) | collective-permute-done | bytes 147488 | tf_op jit(solution)/shard_map/ppermute | solution.py:145
  354.8 2.6 collective-permute-done.72
  357.5 5.9 %collective-permute-start.73 = (bf16[192,768]{1,0:T(8,128)(2,1)S(1)}, bf16[192,768]{1,0:T(8,128)(2,1)S(1)}, u32[]{:S(2)}, u32[]{:S(2)}) collective-permute-start(bf16[192,768]{1,0:T(8,128)(2,1)S(1)} %pad_maximum_fusion.24), channel_id=1, source_target_pairs={{0,2},{2,0},{4,6},{6,4},{1,3},{3,1},{5,7},{7,5},{8,10},{10,8},{12,... | collective-permute-start | bytes 884744 | tf_op jit(solution)/shard_map/ppermute | solution.py:145
  364.1 3.3 collective-permute-start.63
  367.3 4.0 %collective-permute-done.73 = bf16[192,768]{1,0:T(8,128)(2,1)S(1)} collective-permute-done((bf16[192,768]{1,0:T(8,128)(2,1)S(1)}, bf16[192,768]{1,0:T(8,128)(2,1)S(1)}, u32[]{:S(2)}, u32[]{:S(2)}) %collective-permute-start.73) | collective-permute-done | bytes 294944 | tf_op jit(solution)/shard_map/ppermute | solution.py:145
  371.6 5.0 %collective-permute-done.63 = bf16[48,3072]{1,0:T(8,128)(2,1)S(1)} collective-permute-done((bf16[48,3072]{1,0:T(8,128)(2,1)S(1)}, bf16[48,3072]{1,0:T(8,128)(2,1)S(1)}, u32[]{:S(2)}, u32[]{:S(2)}) %collective-permute-start.63) | collective-permute-done | bytes 294944 | tf_op jit(solution)/shard_map/ppermute | solution.py:145
  (370 shorter events, 127.7 us)
Async XLA Ops:
  2.6 38.0 %collective-permute-start = (bf16[2,48,2304]{2,1,0:T(8,128)(2,1)}, bf16[2,48,2304]{2,1,0:T(8,128)(2,1)S(1)}, u32[]{:S(2)}, u32[]{:S(2)}) collective-permute-start(bf16[2,48,2304]{2,1,0:T(8,128)(2,1)} %dynamic-slice_bitcast_fusion.18), channel_id=1, source_target_pairs={{0,8},{8,0},{16,24},{24,16},{1,9},{9,1},{17,25},{25,17},{2,10},{10... | collective-permute-start | bytes 1327112 | tf_op jit(solution)/shard_map/ppermute | solution.py:145
  5.6 39.3 %collective-permute-start.2 = (bf16[2,48,2304]{2,1,0:T(8,128)(2,1)}, bf16[2,48,2304]{2,1,0:T(8,128)(2,1)S(1)}, u32[]{:S(2)}, u32[]{:S(2)}) collective-permute-start(bf16[2,48,2304]{2,1,0:T(8,128)(2,1)} %dynamic-slice_bitcast_fusion.18), channel_id=1, source_target_pairs={{0,16},{8,24},{16,0},{24,8},{1,17},{9,25},{17,1},{25,9},{2,18},{10... | collective-permute-start | bytes 1327112 | tf_op jit(solution)/shard_map/ppermute | solution.py:145
  40.7 36.0 %collective-permute-start.23 = (bf16[2,192,768]{2,1,0:T(8,128)(2,1)S(1)}, bf16[2,192,768]{2,1,0:T(8,128)(2,1)S(1)}, u32[]{:S(2)}, u32[]{:S(2)}) collective-permute-start(bf16[2,192,768]{2,1,0:T(8,128)(2,1)S(1)} %dynamic-slice_bitcast_fusion.16), channel_id=1, source_target_pairs={{0,8},{8,0},{16,24},{24,16},{1,9},{9,1},{17,25},{25,17},{2,10},{10... | collective-permute-start | bytes 1769480 | tf_op jit(solution)/shard_map/ppermute | solution.py:145
  42.2 36.2 %collective-permute-start.25 = (bf16[2,192,768]{2,1,0:T(8,128)(2,1)S(1)}, bf16[2,192,768]{2,1,0:T(8,128)(2,1)S(1)}, u32[]{:S(2)}, u32[]{:S(2)}) collective-permute-start(bf16[2,192,768]{2,1,0:T(8,128)(2,1)S(1)} %dynamic-slice_bitcast_fusion.16), channel_id=1, source_target_pairs={{0,16},{8,24},{16,0},{24,8},{1,17},{9,25},{17,1},{25,9},{2,18},{10... | collective-permute-start | bytes 1769480 | tf_op jit(solution)/shard_map/ppermute | solution.py:145
  42.7 15.1 %collective-permute-start.9 = (bf16[2,48,768]{2,1,0:T(8,128)(2,1)S(1)}, bf16[2,48,768]{2,1,0:T(8,128)(2,1)S(1)}, u32[]{:S(2)}, u32[]{:S(2)}) collective-permute-start(bf16[2,48,768]{2,1,0:T(8,128)(2,1)S(1)} %dynamic-slice_bitcast_fusion.40), channel_id=1, source_target_pairs={{0,8},{8,0},{16,24},{24,16},{1,9},{9,1},{17,25},{25,17},{2,10},{10... | collective-permute-start | bytes 442376 | tf_op jit(solution)/shard_map/ppermute | solution.py:145
  44.0 17.6 %collective-permute-start.11 = (bf16[2,48,768]{2,1,0:T(8,128)(2,1)S(1)}, bf16[2,48,768]{2,1,0:T(8,128)(2,1)S(1)}, u32[]{:S(2)}, u32[]{:S(2)}) collective-permute-start(bf16[2,48,768]{2,1,0:T(8,128)(2,1)S(1)} %dynamic-slice_bitcast_fusion.40), channel_id=1, source_target_pairs={{0,16},{8,24},{16,0},{24,8},{1,17},{9,25},{17,1},{25,9},{2,18},{10... | collective-permute-start | bytes 442376 | tf_op jit(solution)/shard_map/ppermute | solution.py:145
  44.9 19.7 %collective-permute-start.4 = (bf16[48,2304]{1,0:T(8,128)(2,1)S(1)}, bf16[48,2304]{1,0:T(8,128)(2,1)S(1)}, u32[]{:S(2)}, u32[]{:S(2)}) collective-permute-start(bf16[48,2304]{1,0:T(8,128)(2,1)S(1)} %slice_bitcast_fusion.17), channel_id=1, source_target_pairs={{0,16},{8,24},{16,0},{24,8},{1,17},{9,25},{17,1},{25,9},{2,18},{10... | collective-permute-start | bytes 663560 | tf_op jit(solution)/shard_map/ppermute | solution.py:145
  57.8 7.3 %collective-permute-start.5 = (bf16[48,2304]{1,0:T(8,128)(2,1)S(1)}, bf16[48,2304]{1,0:T(8,128)(2,1)S(1)}, u32[]{:S(2)}, u32[]{:S(2)}) collective-permute-start(bf16[48,2304]{1,0:T(8,128)(2,1)S(1)} %slice_bitcast_fusion.16), channel_id=1, source_target_pairs={{0,8},{8,0},{16,24},{24,16},{1,9},{9,1},{17,25},{25,17},{2,10},{10... | collective-permute-start | bytes 663560 | tf_op jit(solution)/shard_map/ppermute | solution.py:145
  66.0 15.8 %collective-permute-start.16 = (bf16[2,48,3072]{2,1,0:T(8,128)(2,1)S(1)}, bf16[2,48,3072]{2,1,0:T(8,128)(2,1)S(1)}, u32[]{:S(2)}, u32[]{:S(2)}) collective-permute-start(bf16[2,48,3072]{2,1,0:T(8,128)(2,1)S(1)} %dynamic-slice_bitcast_fusion.17), channel_id=1, source_target_pairs={{0,8},{8,0},{16,24},{24,16},{1,9},{9,1},{17,25},{25,17},{2,10},{10... | collective-permute-start | bytes 1769480 | tf_op jit(solution)/shard_map/ppermute | solution.py:145
  69.5 15.1 %collective-permute-start.18 = (bf16[2,48,3072]{2,1,0:T(8,128)(2,1)S(1)}, bf16[2,48,3072]{2,1,0:T(8,128)(2,1)S(1)}, u32[]{:S(2)}, u32[]{:S(2)}) collective-permute-start(bf16[2,48,3072]{2,1,0:T(8,128)(2,1)S(1)} %dynamic-slice_bitcast_fusion.17), channel_id=1, source_target_pairs={{0,16},{8,24},{16,0},{24,8},{1,17},{9,25},{17,1},{25,9},{2,18},{10... | collective-permute-start | bytes 1769480 | tf_op jit(solution)/shard_map/ppermute | solution.py:145
  76.3 9.1 %collective-permute-start.6 = (bf16[2,48,2304]{2,1,0:T(8,128)(2,1)S(1)}, bf16[2,48,2304]{2,1,0:T(8,128)(2,1)S(1)}, u32[]{:S(2)}, u32[]{:S(2)}) collective-permute-start(bf16[2,48,2304]{2,1,0:T(8,128)(2,1)S(1)} %pad_maximum_fusion.18), channel_id=1, source_target_pairs={{0,1},{1,0},{2,3},{3,2},{4,5},{5,4},{6,7},{7,6},{8,9},{9,8},{10,11... | collective-permute-start | bytes 1327112 | tf_op jit(solution)/shard_map/ppermute | solution.py:145
  76.7 32.9 %collective-permute-start.27 = (bf16[192,768]{1,0:T(8,128)(2,1)S(1)}, bf16[192,768]{1,0:T(8,128)(2,1)S(1)}, u32[]{:S(2)}, u32[]{:S(2)}) collective-permute-start(bf16[192,768]{1,0:T(8,128)(2,1)S(1)} %slice_bitcast_fusion.9), channel_id=1, source_target_pairs={{0,16},{8,24},{16,0},{24,8},{1,17},{9,25},{17,1},{25,9},{2,18},{10... | collective-permute-start | bytes 884744 | tf_op jit(solution)/shard_map/ppermute | solution.py:145
  78.5 31.7 %collective-permute-start.28 = (bf16[192,768]{1,0:T(8,128)(2,1)S(1)}, bf16[192,768]{1,0:T(8,128)(2,1)S(1)}, u32[]{:S(2)}, u32[]{:S(2)}) collective-permute-start(bf16[192,768]{1,0:T(8,128)(2,1)S(1)} %slice_bitcast_fusion.8), channel_id=1, source_target_pairs={{0,8},{8,0},{16,24},{24,16},{1,9},{9,1},{17,25},{25,17},{2,10},{10... | collective-permute-start | bytes 884744 | tf_op jit(solution)/shard_map/ppermute | solution.py:145
  81.8 28.5 %collective-permute-start.20 = (bf16[48,3072]{1,0:T(8,128)(2,1)S(1)}, bf16[48,3072]{1,0:T(8,128)(2,1)S(1)}, u32[]{:S(2)}, u32[]{:S(2)}) collective-permute-start(bf16[48,3072]{1,0:T(8,128)(2,1)S(1)} %slice_bitcast_fusion.11), channel_id=1, source_target_pairs={{0,16},{8,24},{16,0},{24,8},{1,17},{9,25},{17,1},{25,9},{2,18},{10... | collective-permute-start | bytes 884744 | tf_op jit(solution)/shard_map/ppermute | solution.py:145
  84.6 26.2 %collective-permute-start.21 = (bf16[48,3072]{1,0:T(8,128)(2,1)S(1)}, bf16[48,3072]{1,0:T(8,128)(2,1)S(1)}, u32[]{:S(2)}, u32[]{:S(2)}) collective-permute-start(bf16[48,3072]{1,0:T(8,128)(2,1)S(1)} %slice_bitcast_fusion.10), channel_id=1, source_target_pairs={{0,8},{8,0},{16,24},{24,16},{1,9},{9,1},{17,25},{25,17},{2,10},{10... | collective-permute-start | bytes 884744 | tf_op jit(solution)/shard_map/ppermute | solution.py:145
  85.4 25.6 %collective-permute-start.24 = (bf16[2,192,768]{2,1,0:T(8,128)(2,1)S(1)}, bf16[2,192,768]{2,1,0:T(8,128)(2,1)S(1)}, u32[]{:S(2)}, u32[]{:S(2)}) collective-permute-start(bf16[2,192,768]{2,1,0:T(8,128)(2,1)S(1)} %collective-permute-done.23), channel_id=1, source_target_pairs={{0,1},{1,0},{2,3},{3,2},{4,5},{5,4},{6,7},{7,6},{8,9},{9,8},{10,11... | collective-permute-start | bytes 1769480 | tf_op jit(solution)/shard_map/ppermute | solution.py:145
  222.1 12.4 %collective-permute-start.45 = (bf16[4,2,48,768]{3,2,1,0:T(8,128)(2,1)S(1)}, bf16[4,2,48,768]{3,2,1,0:T(8,128)(2,1)S(1)}, u32[]{:S(2)}, u32[]{:S(2)}) collective-permute-start(bf16[4,2,48,768]{3,2,1,0:T(8,128)(2,1)S(1)} %dynamic-slice_bitcast_fusion.15), channel_id=1, source_target_pairs={{0,1},{1,0},{2,3},{3,2},{4,5},{5,4},{6,7},{7,6},{8,9},{9,8},{10,11... | collective-permute-start | bytes 1769480 | tf_op jit(solution)/shard_map/ppermute | solution.py:145
  223.1 7.1 %collective-permute-start.40 = (f32[4,2304]{1,0:T(4,128)S(1)}, f32[4,2304]{1,0:T(4,128)S(1)}, u32[]{:S(2)}, u32[]{:S(2)}) collective-permute-start(f32[4,2304]{1,0:T(4,128)S(1)} %concatenate.93), channel_id=1, source_target_pairs={{0,1},{1,0},{2,3},{3,2},{4,5},{5,4},{6,7},{7,6},{8,9},{9,8},{10,11... | collective-permute-start | bytes 110600 | tf_op jit(solution)/shard_map/ppermute | solution.py:145
  233.3 50.2 %collective-permute-start.65 = (bf16[4,2,192,768]{3,2,1,0:T(8,128)(2,1)S(1)}, bf16[4,2,192,768]{3,2,1,0:T(8,128)(2,1)S(1)}, u32[]{:S(2)}, u32[]{:S(2)}) collective-permute-start(bf16[4,2,192,768]{3,2,1,0:T(8,128)(2,1)S(1)} %dynamic-slice_bitcast_fusion), channel_id=1, source_target_pairs={{0,1},{1,0},{2,3},{3,2},{4,5},{5,4},{6,7},{7,6},{8,9},{9,8},{10,11... | collective-permute-start | bytes 7077896 | tf_op jit(solution)/shard_map/ppermute | solution.py:145
  234.2 14.2 %collective-permute-start.42 = (f32[4,2304]{1,0:T(4,128)S(1)}, f32[4,2304]{1,0:T(4,128)S(1)}, u32[]{:S(2)}, u32[]{:S(2)}) collective-permute-start(f32[4,2304]{1,0:T(4,128)S(1)} %add.403), channel_id=1, source_target_pairs={{0,16},{8,24},{16,0},{24,8},{1,17},{9,25},{17,1},{25,9},{2,18},{10... | collective-permute-start | bytes 110600 | tf_op jit(solution)/shard_map/ppermute | solution.py:145
  248.3 38.2 %collective-permute-start.55 = (bf16[4,2,48,3072]{3,2,1,0:T(8,128)(2,1)S(1)}, bf16[4,2,48,3072]{3,2,1,0:T(8,128)(2,1)S(1)}, u32[]{:S(2)}, u32[]{:S(2)}) collective-permute-start(bf16[4,2,48,3072]{3,2,1,0:T(8,128)(2,1)S(1)} %dynamic-slice_bitcast_fusion.1), channel_id=1, source_target_pairs={{0,1},{1,0},{2,3},{3,2},{4,5},{5,4},{6,7},{7,6},{8,9},{9,8},{10,11... | collective-permute-start | bytes 7077896 | tf_op jit(solution)/shard_map/ppermute | solution.py:145
  253.7 14.2 %collective-permute-start.30 = (bf16[4,2,48,2304]{3,2,1,0:T(8,128)(2,1)S(1)}, bf16[4,2,48,2304]{3,2,1,0:T(8,128)(2,1)S(1)}, u32[]{:S(2)}, u32[]{:S(2)}) collective-permute-start(bf16[4,2,48,2304]{3,2,1,0:T(8,128)(2,1)S(1)} %dynamic-slice_bitcast_fusion.2), channel_id=1, source_target_pairs={{0,1},{1,0},{2,3},{3,2},{4,5},{5,4},{6,7},{7,6},{8,9},{9,8},{10,11... | collective-permute-start | bytes 5308424 | tf_op jit(solution)/shard_map/ppermute | solution.py:145
  268.6 12.6 %collective-permute-start.31 = (bf16[2,48,2304]{2,1,0:T(8,128)(2,1)S(1)}, bf16[2,48,2304]{2,1,0:T(8,128)(2,1)S(1)}, u32[]{:S(2)}, u32[]{:S(2)}) collective-permute-start(bf16[2,48,2304]{2,1,0:T(8,128)(2,1)S(1)} %pad_maximum_fusion.19), channel_id=1, source_target_pairs={{0,8},{8,0},{16,24},{24,16},{1,9},{9,1},{17,25},{25,17},{2,10},{10... | collective-permute-start | bytes 1327112 | tf_op jit(solution)/shard_map/ppermute | solution.py:145
  269.9 12.6 %collective-permute-start.33 = (bf16[2,48,2304]{2,1,0:T(8,128)(2,1)S(1)}, bf16[2,48,2304]{2,1,0:T(8,128)(2,1)S(1)}, u32[]{:S(2)}, u32[]{:S(2)}) collective-permute-start(bf16[2,48,2304]{2,1,0:T(8,128)(2,1)S(1)} %pad_maximum_fusion.20), channel_id=1, source_target_pairs={{0,16},{8,24},{16,0},{24,8},{1,17},{9,25},{17,1},{25,9},{2,18},{10... | collective-permute-start | bytes 1327112 | tf_op jit(solution)/shard_map/ppermute | solution.py:145
  281.2 8.0 %collective-permute-start.32 = (bf16[48,2304]{1,0:T(8,128)(2,1)S(1)}, bf16[48,2304]{1,0:T(8,128)(2,1)S(1)}, u32[]{:S(2)}, u32[]{:S(2)}) collective-permute-start(bf16[48,2304]{1,0:T(8,128)(2,1)S(1)} %fusion.25), channel_id=1, source_target_pairs={{0,16},{8,24},{16,0},{24,8},{1,17},{9,25},{17,1},{25,9},{2,18},{10... | collective-permute-start | bytes 663560 | tf_op jit(solution)/shard_map/ppermute | solution.py:145
  282.6 8.4 %collective-permute-start.34 = (bf16[48,2304]{1,0:T(8,128)(2,1)S(1)}, bf16[48,2304]{1,0:T(8,128)(2,1)S(1)}, u32[]{:S(2)}, u32[]{:S(2)}) collective-permute-start(bf16[48,2304]{1,0:T(8,128)(2,1)S(1)} %fusion.22), channel_id=1, source_target_pairs={{0,8},{8,0},{16,24},{24,16},{1,9},{9,1},{17,25},{25,17},{2,10},{10... | collective-permute-start | bytes 663560 | tf_op jit(solution)/shard_map/ppermute | solution.py:145
  284.4 30.6 %collective-permute-start.66 = (bf16[2,192,768]{2,1,0:T(8,128)(2,1)S(1)}, bf16[2,192,768]{2,1,0:T(8,128)(2,1)S(1)}, u32[]{:S(2)}, u32[]{:S(2)}) collective-permute-start(bf16[2,192,768]{2,1,0:T(8,128)(2,1)S(1)} %pad_maximum_fusion.14), channel_id=1, source_target_pairs={{0,8},{8,0},{16,24},{24,16},{1,9},{9,1},{17,25},{25,17},{2,10},{10... | collective-permute-start | bytes 1769480 | tf_op jit(solution)/shard_map/ppermute | solution.py:145
  285.7 30.2 %collective-permute-start.68 = (bf16[2,192,768]{2,1,0:T(8,128)(2,1)S(1)}, bf16[2,192,768]{2,1,0:T(8,128)(2,1)S(1)}, u32[]{:S(2)}, u32[]{:S(2)}) collective-permute-start(bf16[2,192,768]{2,1,0:T(8,128)(2,1)S(1)} %pad_maximum_fusion.15), channel_id=1, source_target_pairs={{0,16},{8,24},{16,0},{24,8},{1,17},{9,25},{17,1},{25,9},{2,18},{10... | collective-permute-start | bytes 1769480 | tf_op jit(solution)/shard_map/ppermute | solution.py:145
  291.2 6.0 %collective-permute-start.35 = (bf16[48,2304]{1,0:T(8,128)(2,1)S(1)}, bf16[48,2304]{1,0:T(8,128)(2,1)S(1)}, u32[]{:S(2)}, u32[]{:S(2)}) collective-permute-start(bf16[48,2304]{1,0:T(8,128)(2,1)S(1)} %dynamic-slice_bitcast_fusion.33), channel_id=1, source_target_pairs={{0,2},{2,0},{4,6},{6,4},{1,3},{3,1},{5,7},{7,5},{8,10},{10,8},{12,... | collective-permute-start | bytes 663560 | tf_op jit(solution)/shard_map/ppermute | solution.py:145
  293.3 24.0 %collective-permute-start.56 = (bf16[2,48,3072]{2,1,0:T(8,128)(2,1)S(1)}, bf16[2,48,3072]{2,1,0:T(8,128)(2,1)S(1)}, u32[]{:S(2)}, u32[]{:S(2)}) collective-permute-start(bf16[2,48,3072]{2,1,0:T(8,128)(2,1)S(1)} %pad_maximum_fusion.10), channel_id=1, source_target_pairs={{0,8},{8,0},{16,24},{24,16},{1,9},{9,1},{17,25},{25,17},{2,10},{10... | collective-permute-start | bytes 1769480 | tf_op jit(solution)/shard_map/ppermute | solution.py:145
  297.3 9.6 %collective-permute-start.36 = (bf16[24,2304]{1,0:T(8,128)(2,1)S(1)}, bf16[24,2304]{1,0:T(8,128)(2,1)S(1)}, u32[]{:S(2)}, u32[]{:S(2)}) collective-permute-start(bf16[24,2304]{1,0:T(8,128)(2,1)S(1)} %dynamic-slice_bitcast_fusion.41), channel_id=1, source_target_pairs={{0,4},{2,6},{4,0},{6,2},{1,5},{3,7},{5,1},{7,3},{8,12},{10,14},{12... | collective-permute-start | bytes 331784 | tf_op jit(solution)/shard_map/ppermute | solution.py:145
  306.9 6.4 %collective-permute-start.37 = (bf16[24,2304]{1,0:T(8,128)(2,1)S(1)}, bf16[24,2304]{1,0:T(8,128)(2,1)S(1)}, u32[]{:S(2)}, u32[]{:S(2)}) collective-permute-start(bf16[24,2304]{1,0:T(8,128)(2,1)S(1)} %fusion.30), channel_id=1, source_target_pairs={{0,4},{2,6},{4,0},{6,2},{1,5},{3,7},{5,1},{7,3},{8,12},{10,14},{12... | collective-permute-start | bytes 331784 | tf_op jit(solution)/shard_map/ppermute | solution.py:145
  307.4 15.6 %collective-permute-start.58 = (bf16[2,48,3072]{2,1,0:T(8,128)(2,1)S(1)}, bf16[2,48,3072]{2,1,0:T(8,128)(2,1)S(1)}, u32[]{:S(2)}, u32[]{:S(2)}) collective-permute-start(bf16[2,48,3072]{2,1,0:T(8,128)(2,1)S(1)} %pad_maximum_fusion.11), channel_id=1, source_target_pairs={{0,16},{8,24},{16,0},{24,8},{1,17},{9,25},{17,1},{25,9},{2,18},{10... | collective-permute-start | bytes 1769480 | tf_op jit(solution)/shard_map/ppermute | solution.py:145
  313.4 10.7 %collective-permute-start.38 = (bf16[48,2304]{1,0:T(8,128)(2,1)S(1)}, bf16[48,2304]{1,0:T(8,128)(2,1)S(1)}, u32[]{:S(2)}, u32[]{:S(2)}) collective-permute-start(bf16[48,2304]{1,0:T(8,128)(2,1)S(1)} %pad_maximum_fusion.25), channel_id=1, source_target_pairs={{0,2},{2,0},{4,6},{6,4},{1,3},{3,1},{5,7},{7,5},{8,10},{10,8},{12,... | collective-permute-start | bytes 663560 | tf_op jit(solution)/shard_map/ppermute | solution.py:145
  315.1 11.1 %collective-permute-start.67 = (bf16[192,768]{1,0:T(8,128)(2,1)S(1)}, bf16[192,768]{1,0:T(8,128)(2,1)S(1)}, u32[]{:S(2)}, u32[]{:S(2)}) collective-permute-start(bf16[192,768]{1,0:T(8,128)(2,1)S(1)} %fusion.11), channel_id=1, source_target_pairs={{0,16},{8,24},{16,0},{24,8},{1,17},{9,25},{17,1},{25,9},{2,18},{10... | collective-permute-start | bytes 884744 | tf_op jit(solution)/shard_map/ppermute | solution.py:145
  316.0 10.3 %collective-permute-start.69 = (bf16[192,768]{1,0:T(8,128)(2,1)S(1)}, bf16[192,768]{1,0:T(8,128)(2,1)S(1)}, u32[]{:S(2)}, u32[]{:S(2)}) collective-permute-start(bf16[192,768]{1,0:T(8,128)(2,1)S(1)} %fusion.8), channel_id=1, source_target_pairs={{0,8},{8,0},{16,24},{24,16},{1,9},{9,1},{17,25},{25,17},{2,10},{10... | collective-permute-start | bytes 884744 | tf_op jit(solution)/shard_map/ppermute | solution.py:145
  317.4 11.9 %collective-permute-start.57 = (bf16[48,3072]{1,0:T(8,128)(2,1)S(1)}, bf16[48,3072]{1,0:T(8,128)(2,1)S(1)}, u32[]{:S(2)}, u32[]{:S(2)}) collective-permute-start(bf16[48,3072]{1,0:T(8,128)(2,1)S(1)} %fusion.18), channel_id=1, source_target_pairs={{0,16},{8,24},{16,0},{24,8},{1,17},{9,25},{17,1},{25,9},{2,18},{10... | collective-permute-start | bytes 884744 | tf_op jit(solution)/shard_map/ppermute | solution.py:145
  323.1 6.8 %collective-permute-start.59 = (bf16[48,3072]{1,0:T(8,128)(2,1)S(1)}, bf16[48,3072]{1,0:T(8,128)(2,1)S(1)}, u32[]{:S(2)}, u32[]{:S(2)}) collective-permute-start(bf16[48,3072]{1,0:T(8,128)(2,1)S(1)} %fusion.15), channel_id=1, source_target_pairs={{0,8},{8,0},{16,24},{24,16},{1,9},{9,1},{17,25},{25,17},{2,10},{10... | collective-permute-start | bytes 884744 | tf_op jit(solution)/shard_map/ppermute | solution.py:145
  324.6 21.7 %collective-permute-start.39 = (bf16[96,2304]{1,0:T(8,128)(2,1)S(1)}, bf16[96,2304]{1,0:T(8,128)(2,1)S(1)}, u32[]{:S(2)}, u32[]{:S(2)}) collective-permute-start(bf16[96,2304]{1,0:T(8,128)(2,1)S(1)} %pad_maximum_fusion.22), channel_id=1, source_target_pairs={{0,1},{1,0},{2,3},{3,2},{4,5},{5,4},{6,7},{7,6},{8,9},{9,8},{10,11... | collective-permute-start | bytes 1327112 | tf_op jit(solution)/shard_map/ppermute | solution.py:145
  326.5 10.2 %collective-permute-start.70 = (bf16[192,768]{1,0:T(8,128)(2,1)S(1)}, bf16[192,768]{1,0:T(8,128)(2,1)S(1)}, u32[]{:S(2)}, u32[]{:S(2)}) collective-permute-start(bf16[192,768]{1,0:T(8,128)(2,1)S(1)} %dynamic-slice_bitcast_fusion.19), channel_id=1, source_target_pairs={{0,2},{2,0},{4,6},{6,4},{1,3},{3,1},{5,7},{7,5},{8,10},{10,8},{12,... | collective-permute-start | bytes 884744 | tf_op jit(solution)/shard_map/ppermute | solution.py:145
  330.1 14.3 %collective-permute-start.60 = (bf16[48,3072]{1,0:T(8,128)(2,1)S(1)}, bf16[48,3072]{1,0:T(8,128)(2,1)S(1)}, u32[]{:S(2)}, u32[]{:S(2)}) collective-permute-start(bf16[48,3072]{1,0:T(8,128)(2,1)S(1)} %dynamic-slice_bitcast_fusion.24), channel_id=1, source_target_pairs={{0,2},{2,0},{4,6},{6,4},{1,3},{3,1},{5,7},{7,5},{8,10},{10,8},{12,... | collective-permute-start | bytes 884744 | tf_op jit(solution)/shard_map/ppermute | solution.py:145
  336.9 9.6 %collective-permute-start.71 = (bf16[96,768]{1,0:T(8,128)(2,1)S(1)}, bf16[96,768]{1,0:T(8,128)(2,1)S(1)}, u32[]{:S(2)}, u32[]{:S(2)}) collective-permute-start(bf16[96,768]{1,0:T(8,128)(2,1)S(1)} %dynamic-slice_bitcast_fusion.38), channel_id=1, source_target_pairs={{0,4},{2,6},{4,0},{6,2},{1,5},{3,7},{5,1},{7,3},{8,12},{10,14},{12... | collective-permute-start | bytes 442376 | tf_op jit(solution)/shard_map/ppermute | solution.py:145
  344.5 10.2 %collective-permute-start.61 = (bf16[24,3072]{1,0:T(8,128)(2,1)S(1)}, bf16[24,3072]{1,0:T(8,128)(2,1)S(1)}, u32[]{:S(2)}, u32[]{:S(2)}) collective-permute-start(bf16[24,3072]{1,0:T(8,128)(2,1)S(1)} %dynamic-slice_bitcast_fusion.39), channel_id=1, source_target_pairs={{0,4},{2,6},{4,0},{6,2},{1,5},{3,7},{5,1},{7,3},{8,12},{10,14},{12... | collective-permute-start | bytes 442376 | tf_op jit(solution)/shard_map/ppermute | solution.py:145
  346.5 11.0 %collective-permute-start.72 = (bf16[96,768]{1,0:T(8,128)(2,1)S(1)}, bf16[96,768]{1,0:T(8,128)(2,1)S(1)}, u32[]{:S(2)}, u32[]{:S(2)}) collective-permute-start(bf16[96,768]{1,0:T(8,128)(2,1)S(1)} %fusion.28), channel_id=1, source_target_pairs={{0,4},{2,6},{4,0},{6,2},{1,5},{3,7},{5,1},{7,3},{8,12},{10,14},{12... | collective-permute-start | bytes 442376 | tf_op jit(solution)/shard_map/ppermute | solution.py:145
  354.8 9.2 %collective-permute-start.62 = (bf16[24,3072]{1,0:T(8,128)(2,1)S(1)}, bf16[24,3072]{1,0:T(8,128)(2,1)S(1)}, u32[]{:S(2)}, u32[]{:S(2)}) collective-permute-start(bf16[24,3072]{1,0:T(8,128)(2,1)S(1)} %fusion.29), channel_id=1, source_target_pairs={{0,4},{2,6},{4,0},{6,2},{1,5},{3,7},{5,1},{7,3},{8,12},{10,14},{12... | collective-permute-start | bytes 442376 | tf_op jit(solution)/shard_map/ppermute | solution.py:145
  357.5 13.8 %collective-permute-start.73 = (bf16[192,768]{1,0:T(8,128)(2,1)S(1)}, bf16[192,768]{1,0:T(8,128)(2,1)S(1)}, u32[]{:S(2)}, u32[]{:S(2)}) collective-permute-start(bf16[192,768]{1,0:T(8,128)(2,1)S(1)} %pad_maximum_fusion.24), channel_id=1, source_target_pairs={{0,2},{2,0},{4,6},{6,4},{1,3},{3,1},{5,7},{7,5},{8,10},{10,8},{12,... | collective-permute-start | bytes 884744 | tf_op jit(solution)/shard_map/ppermute | solution.py:145
  364.1 12.5 %collective-permute-start.63 = (bf16[48,3072]{1,0:T(8,128)(2,1)S(1)}, bf16[48,3072]{1,0:T(8,128)(2,1)S(1)}, u32[]{:S(2)}, u32[]{:S(2)}) collective-permute-start(bf16[48,3072]{1,0:T(8,128)(2,1)S(1)} %pad_maximum_fusion.23), channel_id=1, source_target_pairs={{0,2},{2,0},{4,6},{6,4},{1,3},{3,1},{5,7},{7,5},{8,10},{10,8},{12,... | collective-permute-start | bytes 884744 | tf_op jit(solution)/shard_map/ppermute | solution.py:145
  371.5 6.6 %collective-permute-start.74 = (bf16[384,768]{1,0:T(8,128)(2,1)S(1)}, bf16[384,768]{1,0:T(8,128)(2,1)S(1)}, u32[]{:S(2)}, u32[]{:S(2)}) collective-permute-start(bf16[384,768]{1,0:T(8,128)(2,1)S(1)} %pad_maximum_fusion.17), channel_id=1, source_target_pairs={{0,1},{1,0},{2,3},{3,2},{4,5},{5,4},{6,7},{7,6},{8,9},{9,8},{10,11... | collective-permute-start | bytes 1769480 | tf_op jit(solution)/shard_map/ppermute | solution.py:145
  (53 other events, 409.1 us)
